TPU v7x, 128 devices: a whole 4x4x4 slice. The times are simulated.
128 devices in a mesh: fsdp: 16 (over x_lo, z, core), tp: 8 (over y, x_hi).
Axes of the slice: x: 4 (x_hi: 2, x_lo: 2; x = x_hi * 2 + x_lo), y: 4, z: 4, core: 2. Of those that a mesh axis runs over, the one named last changes fastest.
Arguments:
- attn_out: bfloat16 [16384, 8192], P('fsdp', 'tp'), may hold values from -6 to 6
- out_grad: bfloat16 [16384, 5120], P('fsdp'), may hold values from -6 to 6
- master: float32 [5120, 8192], P('fsdp', 'tp'), may hold values from -0.0625 to 0.0625
- moment_one: float32 [5120, 8192], P('fsdp', 'tp'), may hold values from -0.15625 to 0.15625
- moment_two: float32 [5120, 8192], P('fsdp', 'tp'), may hold values from 1e-05 to 0.001
- query: bfloat16 [128, 8192], P('fsdp', 'tp'), may hold values from -150 to 150
- incoming_key: bfloat16 [128, 1024], P('fsdp', 'tp'), may hold values from -6 to 6
- incoming_value: bfloat16 [128, 1024], P('fsdp', 'tp'), may hold values from -48 to 48
- key_cache: bfloat16 [128, 8, 1024, 128], P('fsdp', 'tp'), may hold values from -6 to 6
- stored_value_cache: bfloat16 [128, 8, 1024, 128], P('fsdp', 'tp'), may hold values from -48 to 48
- cache_lengths: int32 [128], P('fsdp'), may hold values from 256 to 1024, as said below
Outputs:
- master_new: float32 [5120, 8192], P('fsdp', 'tp')
- moment_one_new: float32 [5120, 8192], P('fsdp', 'tp')
- moment_two_new: float32 [5120, 8192], P('fsdp', 'tp')
- decoded: bfloat16 [128, 5120], P('fsdp', 'tp')
Inputs may be any that keep to these rules, and one draw needn't show every extreme that they name: `cache_lengths`: some row has exactly 1024 filled slots.
All inputs are finite; a program needn't handle non-finite values.
Results may differ from a plain program's by a relative error of at most 0.022.
Values may be sent and summed in bfloat16 or wider, within the bound.
A program may use at most 128 MiB of HBM per device.

v0:
```python
import jax
import jax.numpy as jnp
from jax import lax
from jax.sharding import PartitionSpec as P

HEAD_SIZE = 128
CACHE_SLOTS = 1024


beta_one = 0.9
beta_two = 0.95
learn_rate = 0.003
weight_decay = 0.1
adam_eps = 1e-08
bias_one = 1.0 - 0.9**10
bias_two = 1.0 - 0.95**10


def shards(
    attn_out,
    out_grad,
    master,
    moment_one,
    moment_two,
    query,
    incoming_key,
    incoming_value,
    key_cache,
    stored_value_cache,
    cache_lengths,
):
    total_tokens = out_grad.shape[0] * lax.axis_size("fsdp")
    summed = lax.psum_scatter(
        lax.dot_general(
            out_grad, attn_out, (((0,), (0,)), ((), ())), preferred_element_type=jnp.float32
        ).astype(jnp.bfloat16),
        "fsdp",
        scatter_dimension=0,
        tiled=True,
    ).astype(jnp.float32)
    grad = summed / total_tokens
    moment_one_new = beta_one * moment_one + (1.0 - beta_one) * grad
    moment_two_new = beta_two * moment_two + (1.0 - beta_two) * grad * grad
    update = moment_one_new / bias_one / (jnp.sqrt(moment_two_new / bias_two) + adam_eps)
    master_new = master * (1.0 - learn_rate * weight_decay) - learn_rate * update
    weights = master_new.astype(jnp.bfloat16)
    row_count = query.shape[0]
    kv_local = key_cache.shape[1]
    heads_local = query.shape[1] // HEAD_SIZE
    group_index = heads_local // kv_local
    score_scale = 1.0 / HEAD_SIZE**0.5
    query_rows = query.reshape(row_count, kv_local, group_index, HEAD_SIZE)
    cached = (
        jnp.einsum("rgqd,rgcd->rgqc", query_rows, key_cache, preferred_element_type=jnp.float32)
        * score_scale
    )
    slots = jnp.arange(CACHE_SLOTS, dtype=jnp.int32)
    valid = slots[None, :] < cache_lengths[:, None]
    cached = jnp.where(valid[:, None, None, :], cached, -jnp.inf)
    fresh_scores = (
        jnp.einsum(
            "rgqd,rgd->rgq",
            query_rows,
            incoming_key.reshape(row_count, kv_local, HEAD_SIZE),
            preferred_element_type=jnp.float32,
        )
        * score_scale
    )
    top = jnp.maximum(jnp.max(cached, axis=-1), fresh_scores)
    expo_cached = jnp.exp(cached - top[..., None])
    expo_fresh = jnp.exp(fresh_scores - top)
    denom = jnp.sum(expo_cached, axis=-1) + expo_fresh
    probs = (expo_cached / denom[..., None]).astype(jnp.bfloat16)
    fresh_probabilities = (expo_fresh / denom).astype(jnp.bfloat16)
    mixed_output = jnp.einsum(
        "rgqc,rgcd->rgqd", probs, stored_value_cache, preferred_element_type=jnp.float32
    )
    mixed_output = mixed_output + fresh_probabilities.astype(jnp.float32)[
        ..., None
    ] * incoming_value.reshape(row_count, kv_local, 1, HEAD_SIZE).astype(jnp.float32)
    attended = mixed_output.reshape(row_count, heads_local * HEAD_SIZE).astype(jnp.bfloat16)
    partial_rows = lax.dot_general(
        attended,
        lax.all_gather(weights, "fsdp", axis=0, tiled=True),
        (((1,), (1,)), ((), ())),
        preferred_element_type=jnp.float32,
    )
    decoded = lax.psum_scatter(
        partial_rows.astype(jnp.bfloat16), "tp", scatter_dimension=1, tiled=True
    )
    return (master_new, moment_one_new, moment_two_new, decoded)


def solution(mesh):
    placed = (
        P("fsdp", "tp"),
        P("fsdp", None),
        P("fsdp", "tp"),
        P("fsdp", "tp"),
        P("fsdp", "tp"),
        P("fsdp", "tp"),
        P("fsdp", "tp"),
        P("fsdp", "tp"),
        P("fsdp", "tp", None, None),
        P("fsdp", "tp", None, None),
        P("fsdp"),
    )
    return jax.shard_map(
        shards,
        mesh=mesh,
        in_specs=placed,
        out_specs=(P("fsdp", "tp"), P("fsdp", "tp"), P("fsdp", "tp"), P("fsdp", "tp")),
        check_vma=False,
    )
```

profile of v0, /device:TPU:1, one launch (start us, length us, event | category | flops | bytes accessed | tf_op | source)
XLA Modules:
  0.0 263.5 jit_solution(14602679668328730684)
XLA Ops:
  7.2 0.0 copy-start
  7.2 0.0 reduce-scatter.5.cloned.1.call-start
  7.2 1.5 copy-done
  8.8 17.9 %convolution_convert_fusion = bf16[5120,1024]{1,0:T(8,128)(2,1)} fusion(bf16[1024,5120]{1,0:T(8,128)(2,1)} %param.12, bf16[1024,1024]{1,0:T(8,128)(2,1)S(1)} %copy-done), kind=kOutput, calls=%fused_computation | convolution fusion | flops 10742661120 | bytes 23068672 | tf_op jit(solution)/shard_map/dot_general | solution.py:34
  26.6 0.0 copy-start.2
  26.6 0.0 reduce-scatter.5.cloned.1.call-update
  26.7 0.0 copy-start.4
  26.7 0.0 copy-start.5
  26.7 0.0 copy-start.3
  26.7 0.0 copy-start.6
  26.7 0.0 all-gather.2.cloned.1.call-start
  26.8 78.9 %reduce-scatter.5.cloned.1.call-done = bf16[320,1024]{1,0:T(8,128)(2,1)} async-done(((bf16[5120,1024]{1,0:T(8,128)(2,1)}), bf16[320,1024]{1,0:T(8,128)(2,1)}) %reduce-scatter.5.cloned.1.call-update) | async-done | bytes 655376 | tf_op jit(solution)/shard_map/reduce_scatter | solution.py:33
  105.7 0.0 copy-done.2
  105.7 4.8 %fusion.33 = (bf16[320,1024]{1,0:T(8,128)(2,1)}, f32[320,1024]{1,0:T(8,128)}, f32[320,1024]{1,0:T(8,128)}, f32[320,1024]{1,0:T(8,128)}) fusion(f32[320,1024]{1,0:T(8,128)S(1)} %copy-done.2, bf16[320,1024]{1,0:T(8,128)(2,1)} %reduce-scatter.5.cloned.1.call-done, f32[320,1024]{1,0:T(8,128)} %param.14, f32[320,1024]{1,0:T(8,128)} %param.15), kind=kLoop, calls=%fused_computation.35 | loop fusion | flops 5570560 | bytes 9175040 | tf_op jit(solution)/shard_map/convert_element_type | solution.py:46
  110.4 0.0 all-gather.2.cloned.1.call-update
  110.5 0.0 reduce-scatter.7.cloned.1.call-start
  110.5 0.0 copy-done.4
  110.5 0.0 copy-done.5
  110.5 0.1 iota_compare_fusion
  110.6 0.0 copy-done.3
  110.6 0.0 copy-done.6
  110.6 0.1 fusion.27
  110.8 0.0 copy-start.1
  110.8 2.5 fusion.36
  113.2 0.2 fusion.22
  113.4 0.0 copy-done.1
  113.5 0.4 fusion.19
  113.9 61.1 %all-gather.2.cloned.1.call-done = bf16[5120,1024]{1,0:T(8,128)(2,1)} async-done(((bf16[320,1024]{1,0:T(8,128)(2,1)}), bf16[5120,1024]{1,0:T(8,128)(2,1)}) %all-gather.2.cloned.1.call-update) | async-done | bytes 10485776 | tf_op jit(solution)/shard_map/all_gather | solution.py:84
  175.0 6.8 %convolution_convert_fusion.1 = bf16[8,5120]{1,0:T(8,128)(2,1)S(1)} fusion(bf16[5120,1024]{1,0:T(8,128)(2,1)} %all-gather.2.cloned.1.call-done, bf16[1,8,8,128]{3,2,1,0:T(8,128)(2,1)S(1)} %fusion.19), kind=kOutput, calls=%fused_computation.1 | convolution fusion | flops 83927040 | bytes 10584064 | tf_op jit(solution)/shard_map/dot_general | solution.py:82
  181.8 1.5 copy.19
  183.3 0.0 reduce-scatter.7.cloned.1.call-update
  183.3 72.1 %reduce-scatter.7.cloned.1.call-done = bf16[640,8]{1,0:T(8,128)(2,1)} async-done(((bf16[5120,8]{1,0:T(8,128)(2,1)}), bf16[640,8]{1,0:T(8,128)(2,1)}) %reduce-scatter.7.cloned.1.call-update) | async-done | bytes 10256
  255.4 1.6 copy.20
  (3 shorter events, 0.0 us)
Async XLA Ops:
  7.2 1.6 copy-start
  7.2 98.5 %reduce-scatter.5.cloned.1.call-start = ((), (), s32[]{:S(2)}) async-start(), calls=%async_computation.2 | async-start | bytes 11141120 | tf_op jit(solution)/shard_map/reduce_scatter | solution.py:33
  26.6 79.0 %copy-start.2 = (f32[320,1024]{1,0:T(8,128)S(1)}, f32[320,1024]{1,0:T(8,128)}, u32[]{:S(2)}) copy-start(f32[320,1024]{1,0:T(8,128)} %param.13) | copy-start | bytes 3932164
  26.7 83.8 %copy-start.4 = (bf16[8,128]{1,0:T(8,128)(2,1)S(1)}, bf16[8,128]{1,0:T(8,128)(2,1)}, u32[]{:S(2)}) copy-start(bf16[8,128]{1,0:T(8,128)(2,1)} %param.18) | copy-start | bytes 6148
  26.7 83.9 %copy-start.5 = (s32[8]{0:T(128)S(1)}, s32[8]{0:T(128)}, u32[]{:S(2)}) copy-start(s32[8]{0:T(128)} %param.21) | copy-start | bytes 100
  26.7 83.9 %copy-start.3 = (bf16[8,1024]{1,0:T(8,128)(2,1)S(1)}, bf16[8,1024]{1,0:T(8,128)(2,1)}, u32[]{:S(2)}) copy-start(bf16[8,1024]{1,0:T(8,128)(2,1)} %param.16) | copy-start | bytes 49156
  26.7 83.9 %copy-start.6 = (bf16[8,128]{1,0:T(8,128)(2,1)S(1)}, bf16[8,128]{1,0:T(8,128)(2,1)}, u32[]{:S(2)}) copy-start(bf16[8,128]{1,0:T(8,128)(2,1)} %param.17) | copy-start | bytes 6148
  26.7 148.3 %all-gather.2.cloned.1.call-start = ((), (), s32[]{:S(2)}) async-start(), calls=%async_computation.3 | async-start | bytes 11141120 | tf_op jit(solution)/shard_map/all_gather | solution.py:84
  110.5 144.9 %reduce-scatter.7.cloned.1.call-start = ((), (), s32[]{:S(2)}) async-start(), calls=%async_computation.4 | async-start | bytes 1474560
  110.8 2.7 %copy-start.1 = (bf16[8,1,1024,128]{3,2,1,0:T(8,128)(2,1)S(1)}, bf16[8,1,1024,128]{3,2,1,0:T(8,128)(2,1)}, u32[]{:S(2)}) copy-start(bf16[8,1,1024,128]{3,2,1,0:T(8,128)(2,1)} %param.20) | copy-start | bytes 6291460
Sparse Core Ops, SparseCore 0:
  26.8 78.8 reduce-scatter.4
  110.6 64.3 all-gather.1
  183.4 71.8 reduce-scatter.6
where the time goes:
time: 264 us
  waiting for transfers between devices  212 us (80%)
  matrix products  27.7 us (10%)
  between operations  13.8 us (5%)
  other arithmetic  5.07 us (2%)
  local copies, waits for them, and re-layouts  4.7 us (2%)
    reduce_scatter x1, waiting for transfers between devices, shards(): lax.psum_scatter(lax.dot_general(out_grad, attn_out, (((0,), (0,)), ((),...  78.9 us
    unnamed x4, waiting for transfers between devices  72.1 us
    all_gather x1, waiting for transfers between devices, shards(): lax.all_gather(weights, 'fsdp', axis=0, tiled=True)  61.1 us
    dot_general x1, matrix products, shards(): lax.dot_general(out_grad, attn_out, (((0,), (0,)), ((), ())), preferred_e...  17.9 us
    dot_general x1, matrix products, shards(): lax.dot_general(attended, lax.all_gather(weights, 'fsdp', axis=0, tiled=T...  6.78 us
  transfers between devices with their start and end apart: 3, of which 3 were waited for; matrix products, arithmetic and copies ran while one was open for 1% of the time, Pallas kernels for 0%

commit v1 on v0

v1 whole, which is shorter than its diff:
```python
import functools

import jax
import jax.numpy as jnp
from jax import lax
from jax.experimental import pallas as pl
from jax.experimental.pallas import tpu as pltpu
from jax.sharding import PartitionSpec as P

MESH = pl.DeviceIdType.MESH
HEAD_SIZE = 128
CACHE_SLOTS = 1024
TOKENS = 16384

beta_one = 0.9
beta_two = 0.95
learn_rate = 0.003
weight_decay = 0.1
adam_eps = 1e-08
bias_one = 1.0 - 0.9**10
bias_two = 1.0 - 0.95**10

NX, NZ = 2, 4
ROWS = 320
COLS = 1024
X_ROWS = 144
Z_ROWS = ROWS - X_ROWS
ORDER = ((1, 2), (1, 1), (1, 3), (0, 2), (0, 1), (0, 3), (1, 0), (0, 0))
SLOT = {place: slot for slot, place in enumerate(ORDER)}
STREAMS = {"zo": (X_ROWS, Z_ROWS, 96), "zs": (X_ROWS, Z_ROWS, 96), "x": (0, X_ROWS, 64)}


def kernel(
    attn_hbm,
    grad_hbm,
    master_hbm,
    one_hbm,
    two_hbm,
    query_hbm,
    new_key_hbm,
    new_value_hbm,
    keys_hbm,
    values_hbm,
    lengths,
    master_out,
    one_out,
    two_out,
    decoded_ref,
    attn,
    grads,
    part,
    from_core,
    from_x,
    from_x_last,
    zo_near,
    zo_far,
    zs_near,
    zs_far,
    x_near,
    x_far,
    master,
    one,
    two,
    query,
    new_key,
    new_value,
    keys,
    values,
    weights,
    heads,
    mixed,
    fresh,
    attended,
    shares,
    arrived,
    load_sem,
    grad_sem,
    core_sem,
    x_sem,
    z_sem,
    attend_sem,
    share_send,
    share_recv,
    store_sem,
):
    f = lax.axis_index("fsdp")
    t = lax.axis_index("tp")
    x, z, k = f // (2 * NZ), lax.rem(f // 2, NZ), lax.rem(f, 2)

    def at(dx, dz, core):
        return ((lax.rem(x + dx, NX) * NZ + lax.rem(z + dz, NZ)) * 2 + core, t)

    def chip(dx, dz):
        return lax.rem(x + dx, NX) * NZ + lax.rem(z + dz, NZ)

    other_core = at(0, 0, 1 - k)
    other_x = at(1, 0, k)
    up, down = at(0, 1, k), at(0, 3, k)
    own = pl.multiple_of(k * ROWS, 64)
    given = pl.multiple_of((1 - k) * ROWS, 64)

    def load(src, dst, n):
        return pltpu.make_async_copy(src, dst, load_sem.at[n])

    attn_load = load(attn_hbm, attn, 0)
    grad_loads = []
    for slot, (dx, dz) in enumerate(ORDER):
        columns = pl.ds(pl.multiple_of(chip(dx, dz) * 2 * ROWS, 128), 2 * ROWS)
        grad_loads.append(
            pltpu.make_async_copy(grad_hbm.at[:, columns], grads.at[slot], grad_sem.at[slot])
        )
    late_loads = [
        load(src, dst, n + 1)
        for n, (src, dst) in enumerate(
            (
                (query_hbm, query),
                (new_key_hbm, new_key),
                (new_value_hbm, new_value),
                (keys_hbm, keys),
                (values_hbm, values),
                (master_hbm, master),
                (one_hbm, one),
                (two_hbm, two),
            )
        )
    ]
    grad_loads[0].start()
    attn_load.start()
    for copy in grad_loads[1:]:
        copy.start()

    barrier = pltpu.get_barrier_semaphore()

    def greet(device):
        pl.semaphore_signal(barrier, inc=1, device_id=device, device_id_type=MESH)

    greet(other_core)
    for place in range(1, NX * NZ):
        greet(at(place // NZ, place % NZ, k))
    self_share = t == f // 2
    for core in range(2):
        for step in range(8):
            source = (2 * t + core, lax.rem(t + step, 8))
            if step == 0:
                @pl.when(jnp.logical_not(jnp.logical_and(self_share, k == core)))
                def _():
                    greet(source)
            else:
                greet(source)
    for copy in late_loads:
        copy.start()

    def remote(src, dst, send, recv, device):
        return pltpu.make_async_remote_copy(
            src_ref=src, dst_ref=dst, send_sem=send, recv_sem=recv, device_id=device, device_id_type=MESH
        )

    def core_copy(slot):
        return remote(
            part.at[slot, pl.ds(given, ROWS)],
            from_core.at[slot],
            core_sem.at[0, slot],
            core_sem.at[1, slot],
            other_core,
        )

    def rows_of(dx, dz, first, count):
        return part.at[SLOT[dx, dz], pl.ds(pl.multiple_of(own + first, 16), count)]

    def add(dst_ref, slot, first, src_ref, src_first, count):
        @pl.loop(0, count // 16)
        def _(n):
            rows = pl.ds(pl.multiple_of(first + n * 16, 16), 16)
            dst_ref[slot, rows, :] = (
                dst_ref[slot, rows, :] + src_ref[pl.ds(pl.multiple_of(src_first + n * 16, 16), 16), :]
            )

    def add_own(dx, dz, first, src_ref, src_first, count):
        add(part, SLOT[dx, dz], own + first, src_ref, src_first, count)

    over_x = [
        remote(rows_of(1, dz, 0, X_ROWS), from_x.at[dz], x_sem.at[0, dz], x_sem.at[1, dz], other_x)
        for dz in range(NZ)
    ]
    last_x = remote(
        rows_of(1, 0, X_ROWS, Z_ROWS), from_x_last, x_sem.at[0, NZ], x_sem.at[1, NZ], other_x
    )

    class Stream:
        def __init__(self, number, name, dx, near, far):
            first, count, cut = STREAMS[name]
            self.first, self.count, self.cut = first, count, cut
            self.dx, self.near, self.far = dx, near, far

            def send(dz, begin, size, dst, n, device):
                return remote(
                    rows_of(dx, dz, first + begin, size),
                    dst,
                    z_sem.at[0, number, n],
                    z_sem.at[1, number, n],
                    device,
                )

            rest = count - cut
            self.far_up = send(2, 0, cut, far.at[pl.ds(0, cut)], 0, up)
            self.far_down = send(2, cut, rest, far.at[pl.ds(cut, rest)], 1, down)
            self.up_free = send(1, cut, rest, near.at[0, pl.ds(cut, rest)], 2, up)
            self.up_late = send(1, 0, cut, near.at[0, pl.ds(0, cut)], 3, up)
            self.down_free = send(3, 0, cut, near.at[1, pl.ds(0, cut)], 4, down)
            self.down_late = send(3, cut, rest, near.at[1, pl.ds(cut, rest)], 5, down)
            self.copies = (
                self.far_up, self.far_down, self.up_free, self.up_late, self.down_free, self.down_late
            )

        def start_far(self):
            self.far_up.start()
            self.far_down.start()

        def pass_far_up(self):
            self.far_up.wait_recv()
            add_own(self.dx, 1, self.first, self.far, 0, self.cut)
            self.up_late.start()

        def pass_far_down(self):
            self.far_down.wait_recv()
            add_own(self.dx, 3, self.first + self.cut, self.far, self.cut, self.count - self.cut)
            self.down_late.start()

        def wait_near(self):
            for copy in self.copies[2:]:
                copy.wait_recv()

        def add_near(self):
            self.wait_near()
            for side in range(2):
                add_own(self.dx, 0, self.first, self.near.at[side], 0, self.count)

    zo = Stream(0, "zo", 1, zo_near, zo_far)
    zs = Stream(1, "zs", 0, zs_near, zs_far)
    xs = Stream(2, "x", 0, x_near, x_far)

    def after_slab(slot):
        dx, dz = ORDER[slot]
        if dx == 1:
            over_x[dz].start()
        stream = zo if dx == 1 else zs
        if dz == 2:
            stream.start_far()
        if dz == 1:
            stream.up_free.start()
        if dz == 3:
            stream.down_free.start()

    def x_far():
        over_x[2].wait_recv()
        add_own(0, 2, 0, from_x.at[2], 0, X_ROWS)
        xs.start_far()

    attn_load.wait()

    @pl.loop(0, len(ORDER) + 1)
    def _(step):
        @pl.when(step < len(ORDER))
        def _():
            pltpu.make_async_copy(
                grad_hbm.at[:, pl.ds(0, 2 * ROWS)], grads.at[step], grad_sem.at[step]
            ).wait()
            part[step] = lax.dot_general(
                grads[step], attn[...], (((0,), (0,)), ((), ())), preferred_element_type=jnp.float32
            ).astype(jnp.bfloat16)

        @pl.when(step == 0)
        def _():
            pl.semaphore_wait(barrier, 8 + 16 - self_share.astype(jnp.int32))

        @pl.when(step < len(ORDER))
        def _():
            core_copy(step).start()

        @pl.when(step > 0)
        def _():
            core_copy(step - 1).wait_recv()
            add(part, step - 1, own, from_core.at[step - 1], 0, ROWS)

        for slot in range(len(ORDER)):
            @pl.when(step == slot + 1)
            def _():
                after_slab(slot)
                if slot == 5:
                    zo.pass_far_up()
                    zo.pass_far_down()
                if slot == 6:
                    x_far()

    for copy in late_loads:
        copy.wait()
    for head in range(8):
        heads[pl.ds(8 * head, 8), :] = query[:, pl.ds(HEAD_SIZE * head, HEAD_SIZE)].astype(jnp.float32)
    fresh[0] = new_key[...].astype(jnp.float32)
    fresh[1] = new_value[...].astype(jnp.float32)
    score_scale = 1.0 / HEAD_SIZE**0.5

    def attend(row):
        own_heads = heads[pl.ds(row, 8, stride=8), :]
        scores = (
            lax.dot_general(
                own_heads.astype(jnp.bfloat16),
                keys[row, 0],
                (((1,), (1,)), ((), ())),
                preferred_element_type=jnp.float32,
            )
            * score_scale
        )
        slots = lax.broadcasted_iota(jnp.int32, (8, CACHE_SLOTS), 1)
        scores = jnp.where(slots < lengths[row], scores, -jnp.inf)
        new_score = (
            jnp.sum(own_heads * fresh[0, pl.ds(row, 1), :], axis=-1, keepdims=True) * score_scale
        )
        top = jnp.maximum(jnp.max(scores, axis=-1, keepdims=True), new_score)
        expo = jnp.exp(scores - top)
        expo_new = jnp.exp(new_score - top)
        total = jnp.sum(expo, axis=-1, keepdims=True) + expo_new
        probs = (expo / total).astype(jnp.bfloat16)
        prob_new = (expo_new / total).astype(jnp.bfloat16).astype(jnp.float32)
        mixed[pl.ds(row, 8, stride=8), :] = (
            jnp.dot(probs, values[row, 0], preferred_element_type=jnp.float32)
            + prob_new * fresh[1, pl.ds(row, 1), :]
        )

    @pl.loop(0, 4)
    def _(row):
        attend(row)

    zo.add_near()
    last_x.start()

    @pl.loop(4, 8)
    def _(row):
        attend(row)

    halves = [
        jnp.concatenate([mixed[pl.ds(8 * head, 8), :] for head in range(4 * half, 4 * half + 4)], axis=1)
        for half in range(2)
    ]
    here = chip(0, 0)
    attended[k, here] = jnp.concatenate(halves, axis=0).astype(jnp.bfloat16)
    gathers = [
        remote(
            attended.at[k, here],
            attended.at[k, here],
            attend_sem.at[0, place],
            attend_sem.at[1, place],
            at(place // NZ, place % NZ, k),
        )
        for place in range(1, NX * NZ)
    ]
    for copy in gathers:
        copy.start()

    over_x[1].wait_recv()
    add_own(0, 1, 0, from_x.at[1], 0, X_ROWS)
    xs.up_free.start()
    zs.pass_far_up()
    zs.pass_far_down()
    xs.pass_far_up()
    over_x[3].wait_recv()
    add_own(0, 3, 0, from_x.at[3], 0, X_ROWS)
    xs.down_free.start()
    xs.pass_far_down()

    for copy in gathers:
        copy.wait_recv()
    swap = remote(
        attended.at[k], attended.at[k], attend_sem.at[0, 0], attend_sem.at[1, 0], other_core
    )
    swap.start()

    def adam(first, count, terms):
        slot = SLOT[0, 0]

        @pl.loop(0, count // 16)
        def _(n):
            begin = pl.multiple_of(n * 16, 16)
            rows = pl.ds(pl.multiple_of(first + begin, 16), 16)
            total = part[slot, pl.ds(pl.multiple_of(own + first + begin, 16), 16), :].astype(jnp.float32)
            for term in terms:
                total = total + term[pl.ds(begin, 16), :].astype(jnp.float32)
            grad = total * (1.0 / TOKENS)
            one_new = beta_one * one[rows, :] + (1.0 - beta_one) * grad
            two_new = beta_two * two[rows, :] + (1.0 - beta_two) * grad * grad
            update = one_new / bias_one / (jnp.sqrt(two_new / bias_two) + adam_eps)
            master_new = master[rows, :] * (1.0 - learn_rate * weight_decay) - learn_rate * update
            one[rows, :] = one_new
            two[rows, :] = two_new
            master[rows, :] = master_new
            weights[rows, :] = master_new.astype(jnp.bfloat16)

    zs.wait_near()
    over_x[0].wait_recv()
    last_x.wait_recv()
    adam(X_ROWS, Z_ROWS, (from_x_last, zs_near.at[0], zs_near.at[1]))
    xs.wait_near()
    adam(0, X_ROWS, (from_x.at[0], x_near.at[0], x_near.at[1]))
    stores = [
        pltpu.make_async_copy(src, dst, store_sem.at[n])
        for n, (src, dst) in enumerate(((master, master_out), (one, one_out), (two, two_out)))
    ]
    for copy in stores:
        copy.start()

    swap.wait_recv()
    every = attended[...].reshape(256, 512)
    products = [
        lax.dot_general(
            every,
            weights[:, pl.ds(512 * half, 512)],
            (((1,), (1,)), ((), ())),
            preferred_element_type=jnp.float32,
        ).reshape(2, 8, 16, ROWS)[:, :, 8 * half : 8 * half + 8, :]
        for half in range(2)
    ]
    shares[...] = products[0] + products[1]

    def share_copy(step):
        target = lax.rem(f + step, 16)
        return remote(
            shares.at[lax.rem(target, 2), target // 2],
            arrived.at[k, t],
            share_send.at[step],
            share_recv.at[k, t],
            (target, f // 2),
        )

    @pl.when(self_share)
    def _():
        pltpu.make_async_copy(shares.at[k, f // 2], arrived.at[k, t], share_recv.at[k, t]).start()

    @pl.when(jnp.logical_not(self_share))
    def _():
        share_copy(0).start()

    for step in range(1, 16):
        share_copy(step).start()
    for core in range(2):
        for group in range(8):
            pltpu.make_async_copy(
                shares.at[0, 0], arrived.at[core, group], share_recv.at[core, group]
            ).wait()
    decoded_ref[...] = jnp.concatenate(
        [jnp.sum(arrived[core], axis=0) for core in range(2)], axis=1
    )

    @pl.when(jnp.logical_not(self_share))
    def _():
        share_copy(0).wait_send()

    for step in range(1, 16):
        share_copy(step).wait_send()
    for slot in range(len(ORDER)):
        core_copy(slot).wait_send()
    for copy in (*over_x, last_x, *zo.copies, *zs.copies, *xs.copies, *gathers, swap):
        copy.wait_send()
    for copy in stores:
        copy.wait()


def shards(*args):
    any_space = pl.BlockSpec(memory_space=pl.ANY)
    bf16, f32 = jnp.bfloat16, jnp.float32
    results = pl.pallas_call(
        kernel,
        out_shape=(
            jax.ShapeDtypeStruct((ROWS, COLS), f32),
            jax.ShapeDtypeStruct((ROWS, COLS), f32),
            jax.ShapeDtypeStruct((ROWS, COLS), f32),
            jax.ShapeDtypeStruct((8, 640), f32),
        ),
        in_specs=[any_space] * 10 + [pl.BlockSpec(memory_space=pltpu.SMEM)],
        out_specs=(any_space,) * 3 + (pl.BlockSpec(memory_space=pltpu.VMEM),),
        scratch_shapes=[
            pltpu.VMEM((1024, COLS), bf16),
            pltpu.VMEM((8, 1024, 2 * ROWS), bf16),
            pltpu.VMEM((8, 2 * ROWS, COLS), bf16),
            pltpu.VMEM((8, ROWS, COLS), bf16),
            pltpu.VMEM((NZ, X_ROWS, COLS), bf16),
            pltpu.VMEM((Z_ROWS, COLS), bf16),
            pltpu.VMEM((2, Z_ROWS, COLS), bf16),
            pltpu.VMEM((Z_ROWS, COLS), bf16),
            pltpu.VMEM((2, Z_ROWS, COLS), bf16),
            pltpu.VMEM((Z_ROWS, COLS), bf16),
            pltpu.VMEM((2, X_ROWS, COLS), bf16),
            pltpu.VMEM((X_ROWS, COLS), bf16),
            pltpu.VMEM((ROWS, COLS), f32),
            pltpu.VMEM((ROWS, COLS), f32),
            pltpu.VMEM((ROWS, COLS), f32),
            pltpu.VMEM((8, 1024), bf16),
            pltpu.VMEM((8, HEAD_SIZE), bf16),
            pltpu.VMEM((8, HEAD_SIZE), bf16),
            pltpu.VMEM((8, 1, CACHE_SLOTS, HEAD_SIZE), bf16),
            pltpu.VMEM((8, 1, CACHE_SLOTS, HEAD_SIZE), bf16),
            pltpu.VMEM((ROWS, COLS), bf16),
            pltpu.VMEM((64, HEAD_SIZE), f32),
            pltpu.VMEM((64, HEAD_SIZE), f32),
            pltpu.VMEM((2, 8, HEAD_SIZE), f32),
            pltpu.VMEM((2, 8, 16, 512), bf16),
            pltpu.VMEM((2, 8, 8, ROWS), f32),
            pltpu.VMEM((2, 8, 8, ROWS), f32),
            pltpu.SemaphoreType.DMA((9,)),
            pltpu.SemaphoreType.DMA((8,)),
            pltpu.SemaphoreType.DMA((2, 8)),
            pltpu.SemaphoreType.DMA((2, NZ + 1)),
            pltpu.SemaphoreType.DMA((2, 3, 6)),
            pltpu.SemaphoreType.DMA((2, 8)),
            pltpu.SemaphoreType.DMA((16,)),
            pltpu.SemaphoreType.DMA((2, 8)),
            pltpu.SemaphoreType.DMA((3,)),
        ],
        compiler_params=pltpu.CompilerParams(
            collective_id=0, has_side_effects=True, vmem_limit_bytes=58 << 20
        ),
        cost_estimate=pl.CostEstimate(
            flops=2 * 1024 * 1024 * 5120, bytes_accessed=24 << 20, transcendentals=1 << 19
        ),
    )(*args)
    return (*results[:3], results[3].astype(jnp.bfloat16))


def solution(mesh):
    placed = (
        P("fsdp", "tp"),
        P("fsdp", None),
        P("fsdp", "tp"),
        P("fsdp", "tp"),
        P("fsdp", "tp"),
        P("fsdp", "tp"),
        P("fsdp", "tp"),
        P("fsdp", "tp"),
        P("fsdp", "tp", None, None),
        P("fsdp", "tp", None, None),
        P("fsdp"),
    )
    return jax.shard_map(
        shards,
        mesh=mesh,
        in_specs=placed,
        out_specs=(P("fsdp", "tp"), P("fsdp", "tp"), P("fsdp", "tp"), P("fsdp", "tp")),
        check_vma=False,
    )
```

time: 264 us -> 72.5 us (0.27)
  waiting for transfers between devices: 212 us -> 0 us
  Pallas kernels: 0 us -> 64.1 us
  matrix products: 27.7 us -> 0 us
  between operations: 13.8 us -> 0.65 us
  other arithmetic: 5.07 us -> 1.33 us
    reduce_scatter x1 -> x0, waiting for transfers between devices: 78.9 us -> none  [shards(): lax.psum_scatter(lax.dot_general(out_grad, attn_out, (((0,), (0,)), ((),...]
    unnamed x4 -> x0, waiting for transfers between devices: 72.1 us -> none
    pallas_call x0 -> x1, Pallas kernels: none -> 64.1 us  [shards(): pl.pallas_call(kernel, out_shape=(jax.ShapeDtypeStruct((ROWS, COLS), f32)...]
    all_gather x1 -> x0, waiting for transfers between devices: 61.1 us -> none  [shards(): lax.all_gather(weights, 'fsdp', axis=0, tiled=True)]
    dot_general x5 -> x0, matrix products: 27.7 us -> none  [the longest x1 17.9 us: shards(): lax.dot_general(out_grad, attn_out, (((0,), (0,)), ((), ())), preferred_e...]
    convert_element_type x3 -> x1, other arithmetic: 4.79 us -> 1.33 us  [shards(): return (*results[:3], results[3].astype(jnp.bfloat16))]
    unnamed x16 -> x7, local copies, waits for them, and re-layouts: 4.7 us -> 5.48 us
  transfers between devices with their start and end apart: 3 -> 0, of which waited for: 3 -> 0; matrix products, arithmetic and copies ran while one was open for 1% -> 0% of each run, Pallas kernels for 0% -> 0%
where the time goes in v1:
time: 72.5 us; the launch traced here: 71.5 us
  Pallas kernels  64.1 us (88%)
  local copies, waits for them, and re-layouts  5.48 us (8%)
  other arithmetic  1.33 us (2%)
    pallas_call x1, Pallas kernels, shards(): pl.pallas_call(kernel, out_shape=(jax.ShapeDtypeStruct((ROWS, COLS), f32)...  64.1 us
    unnamed x7, local copies, waits for them, and re-layouts  5.48 us

profile of v1, /device:TPU:1, one launch (start us, length us, event | category | flops | bytes accessed | tf_op | source)
XLA Modules:
  0.0 71.5 jit_solution(259185848866886550)
XLA Ops:
  0.6 64.1 %shard_map.138 = (f32[320,1024]{1,0:T(8,128)}, f32[320,1024]{1,0:T(8,128)}, f32[320,1024]{1,0:T(8,128)}, f32[8,640]{1,0:T(8,128)}) custom-call(bf16[1024,1024]{1,0:T(8,128)(2,1)} %attn_hbm.1, bf16[1024,5120]{1,0:T(8,128)(2,1)} %grad_hbm.1, f32[320,1024]{1,0:T(8,128)} %master_hbm.1, f32[320,1024]{1,0:T(8,128)} %one_hbm.1, f32[320,1024]{1,0:T(8,128)} %two_hbm.1, ...), custom_call_target="tpu_custom_call" | custom-call | flops 10737418240 | bytes 25165824 | tf_op jit(solution)/shard_map/pallas_call | solution.py:470
  64.7 1.3 %convert_element_type.3 = bf16[8,640]{1,0:T(8,128)(2,1)} convert(f32[8,640]{1,0:T(8,128)} %get-tuple-element.11) | non-fusion elementwise | flops 5120 | bytes 30720 | tf_op jit(solution)/shard_map/convert_element_type | solution.py:525
  66.0 0.0 copy-start.1
  66.0 2.6 %copy.18 = f32[320,1024]{1,0:T(8,128)} copy(f32[320,1024]{1,0:T(8,128)} %get-tuple-element.16) | data formatting | bytes 2621440
  68.7 0.0 copy-done.1
  68.7 0.0 copy-start
  68.7 1.1 %copy.19 = f32[320,1024]{1,0:T(8,128)} copy(f32[320,1024]{1,0:T(8,128)S(1)} %copy-done.1) | data formatting | bytes 2621440
  69.7 0.7 %copy-done = f32[320,1024]{1,0:T(8,128)S(1)} copy-done((f32[320,1024]{1,0:T(8,128)S(1)}, f32[320,1024]{1,0:T(8,128)}, u32[]{:S(2)}) %copy-start) | copy-done | bytes 1310744
  70.5 1.1 %copy.20 = f32[320,1024]{1,0:T(8,128)} copy(f32[320,1024]{1,0:T(8,128)S(1)} %copy-done) | data formatting | bytes 2621440
Async XLA Ops:
  66.0 2.6 %copy-start.1 = (f32[320,1024]{1,0:T(8,128)S(1)}, f32[320,1024]{1,0:T(8,128)}, u32[]{:S(2)}) copy-start(f32[320,1024]{1,0:T(8,128)} %get-tuple-element.17) | copy-start | bytes 3932164
  68.7 1.8 %copy-start = (f32[320,1024]{1,0:T(8,128)S(1)}, f32[320,1024]{1,0:T(8,128)}, u32[]{:S(2)}) copy-start(f32[320,1024]{1,0:T(8,128)} %get-tuple-element.18) | copy-start | bytes 3932164

commit v2 on v1

v2 whole, which is shorter than its diff:
```python
import jax
import jax.numpy as jnp
from jax import lax
from jax.experimental import pallas as pl
from jax.experimental.pallas import tpu as pltpu
from jax.sharding import PartitionSpec as P

MESH = pl.DeviceIdType.MESH
HEAD_SIZE = 128
CACHE_SLOTS = 1024
TOKENS = 16384

beta_one = 0.9
beta_two = 0.95
learn_rate = 0.003
weight_decay = 0.1
adam_eps = 1e-08
bias_one = 1.0 - 0.9**10
bias_two = 1.0 - 0.95**10

NX, NZ = 2, 4
ROWS = 320
COLS = 1024
HALF = COLS // 2
X_ROWS = 144
Z_ROWS = ROWS - X_ROWS
PADDED = 384
ORDER = ((1, 2), (1, 1), (1, 3), (0, 2), (0, 1), (0, 3), (1, 0), (0, 0))
SLABS = len(ORDER)
STEPS = 2 * SLABS
SLOT = {place: slot for slot, place in enumerate(ORDER)}
STREAMS = ((1, X_ROWS, Z_ROWS, 96), (0, X_ROWS, Z_ROWS, 96), (0, 0, X_ROWS, 64))


def kernel(
    attn_hbm,
    grad_hbm,
    master_hbm,
    one_hbm,
    two_hbm,
    query_hbm,
    new_key_hbm,
    new_value_hbm,
    keys_hbm,
    values_hbm,
    lengths_hbm,
    master_out,
    one_out,
    two_out,
    decoded_out,
    attn,
    grads,
    part,
    from_core,
    from_x,
    from_x_last,
    zo_near,
    zo_far,
    zs_near,
    zs_far,
    xs_near,
    xs_far,
    master,
    one,
    two,
    query,
    new_key,
    new_value,
    keys,
    values,
    lengths,
    weights,
    heads,
    mixed,
    fresh,
    attended,
    shares,
    arrived,
    totals,
    decoded,
    load_sem,
    attn_sem,
    grad_sem,
    core_sem,
    x_sem,
    z_sem,
    attend_sem,
    share_sem,
    send_sem,
):
    f = lax.axis_index("fsdp")
    t = lax.axis_index("tp")
    x, z, k = f // (2 * NZ), lax.rem(f // 2, NZ), lax.rem(f, 2)
    y, x_hi = t // 2, lax.rem(t, 2)
    z_summed = lax.rem(z + 2 + y - f // 4 + 8, NZ)

    def chip(dx, dz):
        return lax.rem(x + dx, NX) * NZ + lax.rem(z + dz, NZ)

    def at(dx, dz, core):
        return (chip(dx, dz) * 2 + core, t)

    other_core = at(0, 0, 1 - k)
    other_x = at(1, 0, k)
    up, down = at(0, 1, k), at(0, 3, k)
    own = pl.multiple_of(k * ROWS, 64)
    given = pl.multiple_of((1 - k) * ROWS, 64)

    attn_loads = [
        pltpu.make_async_copy(attn_hbm.at[:, pl.ds(HALF * half, HALF)], attn.at[half], attn_sem.at[half])
        for half in range(2)
    ]
    grad_loads = []
    for slot, (dx, dz) in enumerate(ORDER):
        columns = pl.ds(pl.multiple_of(chip(dx, dz) * 2 * ROWS, 128), 2 * ROWS)
        grad_loads.append(
            pltpu.make_async_copy(grad_hbm.at[:, columns], grads.at[slot], grad_sem.at[slot])
        )
    late_loads = [
        pltpu.make_async_copy(src, dst, load_sem.at[n])
        for n, (src, dst) in enumerate(
            (
                (query_hbm, query),
                (new_key_hbm, new_key),
                (new_value_hbm, new_value),
                (lengths_hbm, lengths),
                (keys_hbm, keys),
                (values_hbm, values),
                (master_hbm, master),
                (one_hbm, one),
                (two_hbm, two),
            )
        )
    ]
    grad_loads[0].start()
    attn_loads[0].start()

    barrier = pltpu.get_barrier_semaphore()

    def greet(device):
        pl.semaphore_signal(barrier, inc=1, device_id=device, device_id_type=MESH)

    greet(other_core)
    for place in range(1, NX * NZ):
        greet(at(place // NZ, place % NZ, k))
    for step in range(1, 4):
        greet((f, lax.rem(y + step, 4) * 2 + x_hi))
    y_from = lax.rem(z - lax.rem(t, NZ) + 2 + y + 4, 4)
    for core in range(2):
        for side in range(2):
            greet((2 * t + core, y_from * 2 + side))
    grad_loads[1].start()

    def remote(src, dst, send, recv, device):
        return pltpu.make_async_remote_copy(
            src_ref=src, dst_ref=dst, send_sem=send, recv_sem=recv, device_id=device, device_id_type=MESH
        )

    def wait_bytes(ref, sem):
        pltpu.make_async_copy(ref, ref, sem).wait()

    def core_copy(step):
        return remote(
            part.at[step, pl.ds(given, ROWS)],
            from_core.at[step],
            send_sem.at[0],
            core_sem.at[step],
            other_core,
        )

    def own_rows(half, dx, dz, first, count):
        rows = pl.ds(pl.multiple_of(own + first, 16), count)
        return part.at[half * SLABS + SLOT[dx, dz], rows]

    def add_own(half, dx, dz, first, src, begin, count):
        ref = own_rows(half, dx, dz, first, count)
        ref[...] = ref[...] + src[pl.ds(begin, count), :]

    over_x = [
        [
            remote(
                own_rows(half, 1, dz, 0, X_ROWS),
                from_x.at[half, dz],
                send_sem.at[1],
                x_sem.at[half, dz],
                other_x,
            )
            for dz in range(NZ)
        ]
        for half in range(2)
    ]
    last_x = [
        remote(
            own_rows(half, 1, 0, X_ROWS, Z_ROWS),
            from_x_last.at[half],
            send_sem.at[2],
            x_sem.at[half, NZ],
            other_x,
        )
        for half in range(2)
    ]

    class Stream:
        def __init__(self, half, number, near, far):
            dx, first, count, cut = STREAMS[number]
            rest = count - cut
            self.half, self.dx, self.first, self.count, self.cut, self.rest = half, dx, first, count, cut, rest
            self.near, self.far = near.at[half], far.at[half]

            def send(dz, begin, size, dst, n, device):
                return remote(
                    own_rows(half, dx, dz, first + begin, size),
                    dst,
                    send_sem.at[3 + 2 * number + n // 2],
                    z_sem.at[half, number, n],
                    device,
                )

            near, far = self.near, self.far
            self.far_up = send(2, 0, cut, far.at[pl.ds(0, cut)], 0, up)
            self.far_down = send(2, cut, rest, far.at[pl.ds(cut, rest)], 1, down)
            self.up_free = send(1, cut, rest, near.at[0, pl.ds(cut, rest)], 2, up)
            self.up_late = send(1, 0, cut, near.at[0, pl.ds(0, cut)], 2, up)
            self.down_free = send(3, 0, cut, near.at[1, pl.ds(0, cut)], 2, down)
            self.down_late = send(3, cut, rest, near.at[1, pl.ds(cut, rest)], 2, down)
            self.near_sem = z_sem.at[half, number, 2]

        def start_far(self):
            self.far_up.start()
            self.far_down.start()

        def pass_far(self):
            self.far_up.wait_recv()
            add_own(self.half, self.dx, 1, self.first, self.far, 0, self.cut)
            self.up_late.start()
            self.far_down.wait_recv()
            add_own(self.half, self.dx, 3, self.first + self.cut, self.far, self.cut, self.rest)
            self.down_late.start()

        def wait_near(self):
            wait_bytes(self.near, self.near_sem)

    zo = [Stream(half, 0, zo_near, zo_far) for half in range(2)]
    zs = [Stream(half, 1, zs_near, zs_far) for half in range(2)]
    xs = [Stream(half, 2, xs_near, xs_far) for half in range(2)]

    def send_slab(step):
        half, (dx, dz) = step // SLABS, ORDER[step % SLABS]
        if dx == 1:
            over_x[half][dz].start()
        stream = zo[half] if dx == 1 else zs[half]
        if dz == 2:
            stream.start_far()
        if dz == 1:
            stream.up_free.start()
        if dz == 3:
            stream.down_free.start()

    def add_x(half, dz):
        over_x[half][dz].wait_recv()
        add_own(half, 0, dz, 0, from_x.at[half, dz], 0, X_ROWS)

    def x_far(half):
        add_x(half, 2)
        xs[half].start_far()

    def x_up(half):
        add_x(half, 1)
        xs[half].up_free.start()

    def x_down(half):
        add_x(half, 3)
        xs[half].down_free.start()

    def send_last(half):
        zo[half].wait_near()
        ref = own_rows(half, 1, 0, X_ROWS, Z_ROWS)
        ref[...] = ref[...] + zo_near[half, 0] + zo_near[half, 1]
        last_x[half].start()

    def split_heads():
        for copy in late_loads[:6]:
            copy.wait()
        for head in range(8):
            heads[pl.ds(8 * head, 8), :] = query[:, pl.ds(HEAD_SIZE * head, HEAD_SIZE)].astype(jnp.float32)
        fresh[0] = new_key[...].astype(jnp.float32)
        fresh[1] = new_value[...].astype(jnp.float32)

    score_scale = 1.0 / HEAD_SIZE**0.5

    def attend(row):
        own_heads = heads[pl.ds(row, 8, stride=8), :]
        scores = (
            lax.dot_general(
                own_heads.astype(jnp.bfloat16),
                keys[row, 0],
                (((1,), (1,)), ((), ())),
                preferred_element_type=jnp.float32,
            )
            * score_scale
        )
        slots = lax.broadcasted_iota(jnp.int32, (8, CACHE_SLOTS), 1)
        scores = jnp.where(slots < lengths[row], scores, -jnp.inf)
        new_score = (
            jnp.sum(own_heads * fresh[0, pl.ds(row, 1), :], axis=-1, keepdims=True) * score_scale
        )
        top = jnp.maximum(jnp.max(scores, axis=-1, keepdims=True), new_score)
        expo = jnp.exp(scores - top)
        expo_new = jnp.exp(new_score - top)
        total = jnp.sum(expo, axis=-1, keepdims=True) + expo_new
        probs = (expo / total).astype(jnp.bfloat16)
        prob_new = (expo_new / total).astype(jnp.bfloat16).astype(jnp.float32)
        mixed[pl.ds(row, 8, stride=8), :] = (
            jnp.dot(probs, values[row, 0], preferred_element_type=jnp.float32)
            + prob_new * fresh[1, pl.ds(row, 1), :]
        )

    here = chip(0, 0)
    gathers = [
        remote(
            attended.at[k, here],
            attended.at[k, here],
            attend_sem.at[0],
            attend_sem.at[1],
            at(place // NZ, place % NZ, k),
        )
        for place in range(1, NX * NZ)
    ]
    swap = remote(
        attended.at[k], attended.at[k], attend_sem.at[2], attend_sem.at[3], other_core
    )

    def send_attended():
        halves = [
            jnp.concatenate(
                [mixed[pl.ds(8 * head, 8), :] for head in range(4 * half, 4 * half + 4)], axis=1
            )
            for half in range(2)
        ]
        attended[k, here] = jnp.concatenate(halves, axis=0).astype(jnp.bfloat16)
        for copy in gathers:
            copy.start()

    first_row = 3
    after = {
        4: [zo[0].pass_far],
        2: [split_heads],
        5: [lambda: x_far(0)],
        8: [lambda: x_up(0), zs[0].pass_far],
        10: [lambda: send_last(0)],
        11: [lambda: x_down(0), send_attended],
        13: [xs[0].pass_far],
    }

    @pl.loop(0, STEPS + 1)
    def _(step):
        @pl.when(step < SLABS)
        def _():
            pltpu.make_async_copy(
                grad_hbm.at[:, pl.ds(0, 2 * ROWS)], grads.at[step], grad_sem.at[step]
            ).wait()

        for half in range(2):
            @pl.when(step == half * SLABS)
            def _():
                attn_loads[half].wait()

        for slot in range(2, SLABS):
            @pl.when(step == slot - 2)
            def _():
                grad_loads[slot].start()
                if slot == 2:
                    for copy in late_loads[:6]:
                        copy.start()
                if slot == 4:
                    attn_loads[1].start()
                if slot == 6:
                    for copy in late_loads[6:]:
                        copy.start()

        @pl.when(step < STEPS)
        def _():
            part[step] = lax.dot_general(
                grads[lax.rem(step, SLABS)],
                attn[step // SLABS],
                (((0,), (0,)), ((), ())),
                preferred_element_type=jnp.float32,
            ).astype(jnp.bfloat16)

        @pl.when(step == 0)
        def _():
            pl.semaphore_wait(barrier, 1 + 7 + 3 + 4)

        @pl.when(step < STEPS)
        def _():
            core_copy(step).start()

        @pl.when(step > 0)
        def _():
            done = step - 1
            core_copy(done).wait_recv()
            rows = pl.ds(own, ROWS)
            part[done, rows, :] = part[done, rows, :] + from_core[done]

        for done in range(STEPS):
            @pl.when(step == done + 1)
            def _():
                send_slab(done)
                for action in after.get(done, ()):
                    action()

        @pl.when(jnp.logical_and(step > first_row, step <= first_row + 8))
        def _():
            attend(step - first_row - 1)

    x_far(1)
    zo[1].pass_far()
    x_up(1)
    zs[1].pass_far()
    x_down(1)
    weights[:, pl.ds(ROWS, PADDED - ROWS), :] = jnp.zeros((2, PADDED - ROWS, HALF), jnp.bfloat16)
    for copy in late_loads[6:]:
        copy.wait()

    def adam(half, first, count, terms):
        columns = pl.ds(HALF * half, HALF)

        @pl.loop(0, count // 16)
        def _(n):
            begin = pl.multiple_of(n * 16, 16)
            rows = pl.ds(pl.multiple_of(first + begin, 16), 16)
            mine = pl.ds(pl.multiple_of(own + first + begin, 16), 16)
            total = part[half * SLABS + SLOT[0, 0], mine, :].astype(jnp.float32)
            for term in terms:
                total = total + term[pl.ds(begin, 16), :].astype(jnp.float32)
            grad = total * (1.0 / TOKENS)
            one_new = beta_one * one[rows, columns] + (1.0 - beta_one) * grad
            two_new = beta_two * two[rows, columns] + (1.0 - beta_two) * grad * grad
            update = (one_new * (1.0 / bias_one)) / (jnp.sqrt(two_new * (1.0 / bias_two)) + adam_eps)
            master_new = master[rows, columns] * (1.0 - learn_rate * weight_decay) - learn_rate * update
            one_out[rows, columns] = one_new
            two_out[rows, columns] = two_new
            master_out[rows, columns] = master_new
            weights[half, rows, :] = master_new.astype(jnp.bfloat16)

    def adam_x(half):
        xs[half].wait_near()
        over_x[half][0].wait_recv()
        adam(half, 0, X_ROWS, (from_x.at[half, 0], xs_near.at[half, 0], xs_near.at[half, 1]))

    def adam_z(half):
        zs[half].wait_near()
        last_x[half].wait_recv()
        adam(half, X_ROWS, Z_ROWS, (from_x_last.at[half], zs_near.at[half, 0], zs_near.at[half, 1]))

    def product(half):
        return lax.dot_general(
            attended[...].reshape(256, HALF),
            weights[half],
            (((1,), (1,)), ((), ())),
            preferred_element_type=jnp.float32,
        ).reshape(2, 8, 16, PADDED)[:, :, 8 * half : 8 * half + 8, :]

    adam_x(0)
    send_last(1)
    xs[1].pass_far()
    wait_bytes(attended.at[k, pl.ds(0, 7)], attend_sem.at[1])
    swap.start()
    adam_z(0)
    swap.wait_recv()
    share = product(0)
    adam_x(1)
    adam_z(1)
    share = share + product(1)

    for place in range(NZ):
        shares[place] = jnp.concatenate(
            [share[core, dx * NZ + place] for dx in range(NX) for core in range(2)], axis=0
        ).astype(jnp.bfloat16)
    for step in range(1, 4):
        remote(
            shares.at[lax.rem(z_summed + step, NZ)],
            arrived.at[step - 1],
            share_sem.at[0],
            share_sem.at[1],
            (f, lax.rem(y + step, 4) * 2 + x_hi),
        ).start()
    wait_bytes(arrived, share_sem.at[1])
    total = shares[z_summed].astype(jnp.float32)
    for step in range(3):
        total = total + arrived[step].astype(jnp.float32)
    totals[...] = total
    for dx in range(NX):
        for core in range(2):
            remote(
                totals.at[pl.ds(8 * (2 * dx + core), 8)],
                decoded.at[k, x_hi],
                share_sem.at[2],
                share_sem.at[3],
                ((dx * NZ + z_summed) * 2 + core, f // 2),
            ).start()

    wait_bytes(from_core, send_sem.at[0])
    wait_bytes(from_x, send_sem.at[1])
    wait_bytes(from_x_last, send_sem.at[2])
    for number, (near, far) in enumerate(((zo_near, zo_far), (zs_near, zs_far), (xs_near, xs_far))):
        wait_bytes(far, send_sem.at[3 + 2 * number])
        wait_bytes(near, send_sem.at[4 + 2 * number])
    wait_bytes(attended.at[k, pl.ds(0, 7)], attend_sem.at[0])
    swap.wait_send()
    wait_bytes(arrived, share_sem.at[0])
    wait_bytes(decoded, share_sem.at[2])
    wait_bytes(decoded, share_sem.at[3])
    decoded_out[...] = decoded[:, 0] + decoded[:, 1]


def write_kernel(master, one, two, decoded, master_out, one_out, two_out, decoded_out, rounded, sems):
    stores = [
        pltpu.make_async_copy(src, dst, sems.at[n])
        for n, (src, dst) in enumerate(((master, master_out), (one, one_out), (two, two_out)))
    ]
    for copy in stores:
        copy.start()
    rounded[...] = jnp.concatenate(
        [decoded[core, :, :ROWS] for core in range(2)], axis=1
    ).astype(jnp.bfloat16)
    stores.append(pltpu.make_async_copy(rounded, decoded_out, sems.at[3]))
    stores[3].start()
    for copy in stores:
        copy.wait()


def shards(*args):
    bf16, f32 = jnp.bfloat16, jnp.float32
    vmem = pl.BlockSpec(memory_space=pltpu.VMEM)
    anywhere = pl.BlockSpec(memory_space=pl.ANY)
    results = pl.pallas_call(
        kernel,
        out_shape=(
            pltpu.VMEM((ROWS, COLS), f32),
            pltpu.VMEM((ROWS, COLS), f32),
            pltpu.VMEM((ROWS, COLS), f32),
            pltpu.VMEM((2, 8, PADDED), f32),
        ),
        in_specs=[anywhere] * 11,
        out_specs=(vmem,) * 4,
        scratch_shapes=[
            pltpu.VMEM((2, 1024, HALF), bf16),
            pltpu.VMEM((SLABS, 1024, 2 * ROWS), bf16),
            pltpu.VMEM((STEPS, 2 * ROWS, HALF), bf16),
            pltpu.VMEM((STEPS, ROWS, HALF), bf16),
            pltpu.VMEM((2, NZ, X_ROWS, HALF), bf16),
            pltpu.VMEM((2, Z_ROWS, HALF), bf16),
            pltpu.VMEM((2, 2, Z_ROWS, HALF), bf16),
            pltpu.VMEM((2, Z_ROWS, HALF), bf16),
            pltpu.VMEM((2, 2, Z_ROWS, HALF), bf16),
            pltpu.VMEM((2, Z_ROWS, HALF), bf16),
            pltpu.VMEM((2, 2, X_ROWS, HALF), bf16),
            pltpu.VMEM((2, X_ROWS, HALF), bf16),
            pltpu.VMEM((ROWS, COLS), f32),
            pltpu.VMEM((ROWS, COLS), f32),
            pltpu.VMEM((ROWS, COLS), f32),
            pltpu.VMEM((8, 1024), bf16),
            pltpu.VMEM((8, HEAD_SIZE), bf16),
            pltpu.VMEM((8, HEAD_SIZE), bf16),
            pltpu.VMEM((8, 1, CACHE_SLOTS, HEAD_SIZE), bf16),
            pltpu.VMEM((8, 1, CACHE_SLOTS, HEAD_SIZE), bf16),
            pltpu.SMEM((8,), jnp.int32),
            pltpu.VMEM((2, PADDED, HALF), bf16),
            pltpu.VMEM((64, HEAD_SIZE), f32),
            pltpu.VMEM((64, HEAD_SIZE), f32),
            pltpu.VMEM((2, 8, HEAD_SIZE), f32),
            pltpu.VMEM((2, 8, 16, HALF), bf16),
            pltpu.VMEM((NZ, 32, PADDED), bf16),
            pltpu.VMEM((3, 32, PADDED), bf16),
            pltpu.VMEM((32, PADDED), f32),
            pltpu.VMEM((2, 2, 8, PADDED), f32),
            pltpu.SemaphoreType.DMA((9,)),
            pltpu.SemaphoreType.DMA((2,)),
            pltpu.SemaphoreType.DMA((SLABS,)),
            pltpu.SemaphoreType.DMA((STEPS,)),
            pltpu.SemaphoreType.DMA((2, NZ + 1)),
            pltpu.SemaphoreType.DMA((2, 3, 3)),
            pltpu.SemaphoreType.DMA((4,)),
            pltpu.SemaphoreType.DMA((4,)),
            pltpu.SemaphoreType.DMA((9,)),
        ],
        compiler_params=pltpu.CompilerParams(
            collective_id=0, has_side_effects=True, vmem_limit_bytes=50 << 20
        ),
        cost_estimate=pl.CostEstimate(
            flops=2 * 1024 * 1024 * 5120, bytes_accessed=24 << 20, transcendentals=1 << 19
        ),
    )(*(pltpu.with_memory_space_constraint(arg, pltpu.HBM) for arg in args))
    return pl.pallas_call(
        write_kernel,
        out_shape=(
            jax.ShapeDtypeStruct((ROWS, COLS), f32),
            jax.ShapeDtypeStruct((ROWS, COLS), f32),
            jax.ShapeDtypeStruct((ROWS, COLS), f32),
            jax.ShapeDtypeStruct((8, 2 * ROWS), bf16),
        ),
        in_specs=[vmem] * 4,
        out_specs=(anywhere,) * 4,
        scratch_shapes=[pltpu.VMEM((8, 2 * ROWS), bf16), pltpu.SemaphoreType.DMA((4,))],
        compiler_params=pltpu.CompilerParams(vmem_limit_bytes=8 << 20),
        cost_estimate=pl.CostEstimate(flops=0, bytes_accessed=8 << 20, transcendentals=0),
    )(*results)


def solution(mesh):
    placed = (
        P("fsdp", "tp"),
        P("fsdp", None),
        P("fsdp", "tp"),
        P("fsdp", "tp"),
        P("fsdp", "tp"),
        P("fsdp", "tp"),
        P("fsdp", "tp"),
        P("fsdp", "tp"),
        P("fsdp", "tp", None, None),
        P("fsdp", "tp", None, None),
        P("fsdp"),
    )
    return jax.shard_map(
        shards,
        mesh=mesh,
        in_specs=placed,
        out_specs=(P("fsdp", "tp"), P("fsdp", "tp"), P("fsdp", "tp"), P("fsdp", "tp")),
        check_vma=False,
    )
```

time: 72.5 us -> 60.1 us (0.83); the launches traced: 71.5 us -> 60 us
  local copies, waits for them, and re-layouts: 5.48 us -> 0 us
  Pallas kernels: 64.1 us -> 59.3 us
  other arithmetic: 1.33 us -> 0 us
    unnamed x7 -> x0, local copies, waits for them, and re-layouts: 5.48 us -> none
    pallas_call x1 -> x2, Pallas kernels: 64.1 us -> 59.3 us  [the longest x1 57.4 us: shards(): pl.pallas_call(kernel, out_shape=(pltpu.VMEM((ROWS, COLS), f32), pltpu.VM...]
    convert_element_type x1 -> x0, other arithmetic: 1.33 us -> none  [shards(): return (*results[:3], results[3].astype(jnp.bfloat16))]
where the time goes in v2:
time: 60.1 us; the launch traced here: 60 us
  Pallas kernels  59.3 us (99%)
  between operations  0.64 us (1%)
    pallas_call x1, Pallas kernels, shards(): pl.pallas_call(kernel, out_shape=(pltpu.VMEM((ROWS, COLS), f32), pltpu.VM...  57.4 us
    pallas_call x1, Pallas kernels, shards(): pl.pallas_call(write_kernel, out_shape=(jax.ShapeDtypeStruct((ROWS, COLS)...  1.96 us

profile of v2, /device:TPU:1, one launch (start us, length us, event | category | flops | bytes accessed | tf_op | source)
XLA Modules:
  0.0 60.0 jit_solution(15811726244423723831)
XLA Ops:
  0.6 57.4 %shard_map.138 = (f32[320,1024]{1,0:T(8,128)S(1)}, f32[320,1024]{1,0:T(8,128)S(1)}, f32[320,1024]{1,0:T(8,128)S(1)}, f32[2,8,384]{2,1,0:T(8,128)S(1)}) custom-call(bf16[1024,1024]{1,0:T(8,128)(2,1)} %attn_hbm.1, bf16[1024,5120]{1,0:T(8,128)(2,1)} %grad_hbm.1, f32[320,1024]{1,0:T(8,128)} %master_hbm.1, f32[320,1024]{1,0:T(8,128)} %one_hbm.1, ...), custom_call_target="tpu_custom_call" | custom-call | flops 10737418240 | bytes 25165824 | tf_op jit(solution)/shard_map/pallas_call | solution.py:537
  58.0 2.0 %shard_map.139 = (f32[320,1024]{1,0:T(8,128)}, f32[320,1024]{1,0:T(8,128)}, f32[320,1024]{1,0:T(8,128)}, bf16[8,640]{1,0:T(8,128)(2,1)}) custom-call(f32[320,1024]{1,0:T(8,128)S(1)} %get-tuple-element.8.master, f32[320,1024]{1,0:T(8,128)S(1)} %get-tuple-element.9.one, f32[320,1024]{1,0:T(8,128)S(1)} %get-tuple-element.10.two, ...), custom_call_target="tpu_custom_call" | custom-call | bytes 8388608 | tf_op jit(solution)/shard_map/pallas_call | solution.py:595

commit v3 on v2

v3 whole, which is shorter than its diff:
```python
import jax
import jax.numpy as jnp
from jax import lax
from jax.experimental import pallas as pl
from jax.experimental.pallas import tpu as pltpu
from jax.sharding import PartitionSpec as P

MESH = pl.DeviceIdType.MESH
HEAD_SIZE = 128
CACHE_SLOTS = 1024
TOKENS = 16384

beta_one = 0.9
beta_two = 0.95
learn_rate = 0.003
weight_decay = 0.1
adam_eps = 1e-08
bias_one = 1.0 - 0.9**10
bias_two = 1.0 - 0.95**10

NX, NZ = 2, 4
ROWS = 320
COLS = 1024
HALF = COLS // 2
EARLY = 256
PADDED = 384
ORDER = ((1, 2), (1, 1), (1, 3), (0, 2), (0, 1), (0, 3), (1, 0), (0, 0))
SLABS = len(ORDER)
SLOT = {place: slot for slot, place in enumerate(ORDER)}
STREAMS = (
    ((1, 112, 144, 80), (0, 112, 144, 80), (0, 0, 112, 48)),
    ((1, 288, 32, 16), (0, 288, 32, 16), (0, 256, 32, 16)),
)
Z_TOTAL = sum(chunk[0][2] for chunk in STREAMS)
X_TOTAL = sum(chunk[2][2] for chunk in STREAMS)
Z_BEGIN = (0, STREAMS[0][0][2])
X_BEGIN = (0, STREAMS[0][2][2])


def kernel(
    attn_hbm,
    grad_hbm,
    master_hbm,
    one_hbm,
    two_hbm,
    query_hbm,
    new_key_hbm,
    new_value_hbm,
    keys_hbm,
    values_hbm,
    lengths_hbm,
    master_out,
    one_out,
    two_out,
    decoded_out,
    attn,
    grads,
    part,
    from_core,
    from_x,
    from_x_last,
    zo_near,
    zo_far,
    zs_near,
    zs_far,
    xs_near,
    xs_far,
    state,
    query,
    new_key,
    new_value,
    caches,
    lengths,
    weights,
    heads,
    mixed,
    fresh,
    attended,
    shares,
    arrived,
    totals,
    decoded,
    late_shares,
    late_arrived,
    load_sem,
    attn_sem,
    grad_sem,
    core_sem,
    x_sem,
    z_sem,
    attend_sem,
    share_sem,
    late_sem,
    send_sem,
):
    f = lax.axis_index("fsdp")
    t = lax.axis_index("tp")
    x, z, k = f // (2 * NZ), lax.rem(f // 2, NZ), lax.rem(f, 2)
    y, x_hi = t // 2, lax.rem(t, 2)
    z_summed = lax.rem(z + 2 + y - f // 4 + 8, NZ)

    def chip(dx, dz):
        return lax.rem(x + dx, NX) * NZ + lax.rem(z + dz, NZ)

    def at(dx, dz, core):
        return (chip(dx, dz) * 2 + core, t)

    other_core = at(0, 0, 1 - k)
    other_x = at(1, 0, k)
    up, down = at(0, 1, k), at(0, 3, k)
    own = pl.multiple_of(k * ROWS, 64)
    given = pl.multiple_of((1 - k) * ROWS, 64)

    attn_loads = [
        pltpu.make_async_copy(
            attn_hbm.at[:, pl.ds(HALF * half, HALF)], attn.at[:, pl.ds(HALF * half, HALF)], attn_sem.at[half]
        )
        for half in range(2)
    ]
    grad_loads = []
    for slot, (dx, dz) in enumerate(ORDER):
        columns = pl.ds(pl.multiple_of(chip(dx, dz) * 2 * ROWS, 128), 2 * ROWS)
        grad_loads.append(
            pltpu.make_async_copy(grad_hbm.at[:, columns], grads.at[slot], grad_sem.at[slot])
        )
    late_loads = [
        pltpu.make_async_copy(src, dst, load_sem.at[n])
        for n, (src, dst) in enumerate(
            (
                (query_hbm, query),
                (new_key_hbm, new_key),
                (new_value_hbm, new_value),
                (lengths_hbm, lengths),
            )
        )
    ]
    late_loads += [
        pltpu.make_async_copy(keys_hbm, caches.at[0], load_sem.at[4]),
        pltpu.make_async_copy(values_hbm, caches.at[1], load_sem.at[4]),
        pltpu.make_async_copy(master_hbm, state.at[0], load_sem.at[5]),
        pltpu.make_async_copy(one_hbm, state.at[1], load_sem.at[5]),
        pltpu.make_async_copy(two_hbm, state.at[2], load_sem.at[5]),
    ]
    first_columns = pl.ds(pl.multiple_of(chip(*ORDER[0]) * 2 * ROWS, 128), 2 * ROWS)
    for piece in range(4):
        rows = pl.ds(256 * piece, 256)
        pltpu.make_async_copy(
            grad_hbm.at[rows, first_columns], grads.at[0, rows], grad_sem.at[0]
        ).start()
        pltpu.make_async_copy(
            attn_hbm.at[rows, pl.ds(0, HALF)], attn.at[rows, pl.ds(0, HALF)], attn_sem.at[0]
        ).start()

    barrier = pltpu.get_barrier_semaphore()

    def greet(device):
        pl.semaphore_signal(barrier, inc=1, device_id=device, device_id_type=MESH)

    greet(other_core)
    for place in range(1, NX * NZ):
        greet(at(place // NZ, place % NZ, k))
    for step in range(1, 4):
        greet((f, lax.rem(y + step, 4) * 2 + x_hi))
    stays = t == f // 2
    for core in range(2):
        for step in range(8):
            source = (2 * t + core, lax.rem(t + step, 8))
            if step == 0:
                @pl.when(jnp.logical_not(jnp.logical_and(stays, k == core)))
                def _():
                    greet(source)
            else:
                greet(source)
    attn_loads[1].start()

    def remote(src, dst, send, recv, device):
        return pltpu.make_async_remote_copy(
            src_ref=src, dst_ref=dst, send_sem=send, recv_sem=recv, device_id=device, device_id_type=MESH
        )

    def wait_bytes(ref, sem):
        pltpu.make_async_copy(ref, ref, sem).wait()

    def core_copy(slot):
        return remote(
            part.at[slot, pl.ds(given, ROWS)],
            from_core.at[slot],
            send_sem.at[0],
            core_sem.at[slot],
            other_core,
        )

    def own_rows(dx, dz, first, count):
        rows = pl.ds(pl.multiple_of(own + first, 16), count)
        return part.at[SLOT[dx, dz], rows]

    def add_own(dx, dz, first, count, *terms):
        ref = own_rows(dx, dz, first, count)
        for begin in range(0, count, 16):
            rows = pl.ds(begin, 16)
            total = ref[rows, :]
            for term in terms:
                total = total + term[rows, :]
            ref[rows, :] = total

    def x_landing(chunk, dz):
        return from_x.at[dz, pl.ds(X_BEGIN[chunk], STREAMS[chunk][2][2])]

    def x_copy(chunk, dz):
        _, first, count, _ = STREAMS[chunk][2]
        return remote(
            own_rows(1, dz, first, count),
            x_landing(chunk, dz),
            send_sem.at[1],
            x_sem.at[chunk, dz],
            other_x,
        )

    over_x = [[x_copy(chunk, dz) for dz in range(NZ)] for chunk in range(2)]

    def z_landing(chunk):
        return from_x_last.at[pl.ds(Z_BEGIN[chunk], STREAMS[chunk][0][2])]

    def last_copy(chunk):
        _, first, count, _ = STREAMS[chunk][0]
        return remote(
            own_rows(1, 0, first, count),
            z_landing(chunk),
            send_sem.at[2],
            x_sem.at[chunk, NZ],
            other_x,
        )

    last_x = [last_copy(chunk) for chunk in range(2)]

    class Stream:
        def __init__(self, chunk, number, near, far):
            dx, first, count, cut = STREAMS[chunk][number]
            rest = count - cut
            place = pl.ds((X_BEGIN if number == 2 else Z_BEGIN)[chunk], count)
            self.dx, self.first, self.count, self.cut, self.rest = dx, first, count, cut, rest
            self.near, self.far = near.at[:, place], far.at[place]

            def send(dz, begin, size, dst, n, device):
                return remote(
                    own_rows(dx, dz, first + begin, size),
                    dst,
                    send_sem.at[3 + 2 * number + n // 2],
                    z_sem.at[chunk, number, n],
                    device,
                )

            near, far = self.near, self.far
            self.far_up = send(2, 0, cut, far.at[pl.ds(0, cut)], 0, up)
            self.far_down = send(2, cut, rest, far.at[pl.ds(cut, rest)], 1, down)
            self.up_free = send(1, cut, rest, near.at[0, pl.ds(cut, rest)], 2, up)
            self.up_late = send(1, 0, cut, near.at[0, pl.ds(0, cut)], 2, up)
            self.down_free = send(3, 0, cut, near.at[1, pl.ds(0, cut)], 2, down)
            self.down_late = send(3, cut, rest, near.at[1, pl.ds(cut, rest)], 2, down)
            self.near_sem = z_sem.at[chunk, number, 2]

        def start_far(self):
            self.far_up.start()
            self.far_down.start()

        def start_free(self):
            self.up_free.start()
            self.down_free.start()

        def pass_far(self):
            self.far_up.wait_recv()
            add_own(self.dx, 1, self.first, self.cut, self.far.at[pl.ds(0, self.cut)])
            self.up_late.start()
            self.far_down.wait_recv()
            add_own(self.dx, 3, self.first + self.cut, self.rest, self.far.at[pl.ds(self.cut, self.rest)])
            self.down_late.start()

        def wait_near(self):
            wait_bytes(self.near, self.near_sem)

    zo = [Stream(chunk, 0, zo_near, zo_far) for chunk in range(2)]
    zs = [Stream(chunk, 1, zs_near, zs_far) for chunk in range(2)]
    xs = [Stream(chunk, 2, xs_near, xs_far) for chunk in range(2)]

    def add_x(chunk, dz):
        over_x[chunk][dz].wait_recv()
        _, first, count, _ = STREAMS[chunk][2]
        add_own(0, dz, first, count, x_landing(chunk, dz))

    def x_far(chunk):
        add_x(chunk, 2)
        xs[chunk].start_far()

    def x_up(chunk):
        add_x(chunk, 1)
        xs[chunk].up_free.start()

    def x_down(chunk):
        add_x(chunk, 3)
        xs[chunk].down_free.start()

    def send_last(chunk):
        stream = zo[chunk]
        stream.wait_near()
        add_own(1, 0, stream.first, stream.count, stream.near.at[0], stream.near.at[1])
        last_x[chunk].start()

    def split_heads():
        for copy in late_loads[:4]:
            copy.wait()
        wait_bytes(caches, load_sem.at[4])
        for head in range(8):
            heads[pl.ds(8 * head, 8), :] = query[:, pl.ds(HEAD_SIZE * head, HEAD_SIZE)].astype(jnp.float32)
        fresh[0] = new_key[...].astype(jnp.float32)
        fresh[1] = new_value[...].astype(jnp.float32)

    score_scale = 1.0 / HEAD_SIZE**0.5

    def attend(row):
        own_heads = heads[pl.ds(row, 8, stride=8), :]
        scores = (
            lax.dot_general(
                own_heads.astype(jnp.bfloat16),
                caches[0, row, 0],
                (((1,), (1,)), ((), ())),
                preferred_element_type=jnp.float32,
            )
            * score_scale
        )
        slots = lax.broadcasted_iota(jnp.int32, (8, CACHE_SLOTS), 1)
        scores = jnp.where(slots < lengths[row], scores, -jnp.inf)
        new_score = (
            jnp.sum(own_heads * fresh[0, pl.ds(row, 1), :], axis=-1, keepdims=True) * score_scale
        )
        top = jnp.maximum(jnp.max(scores, axis=-1, keepdims=True), new_score)
        expo = jnp.exp(scores - top)
        expo_new = jnp.exp(new_score - top)
        total = jnp.sum(expo, axis=-1, keepdims=True) + expo_new
        probs = (expo / total).astype(jnp.bfloat16)
        prob_new = (expo_new / total).astype(jnp.bfloat16).astype(jnp.float32)
        mixed[pl.ds(row, 8, stride=8), :] = (
            jnp.dot(probs, caches[1, row, 0], preferred_element_type=jnp.float32)
            + prob_new * fresh[1, pl.ds(row, 1), :]
        )

    here = chip(0, 0)
    gathers = [
        remote(
            attended.at[k, here],
            attended.at[k, here],
            attend_sem.at[0],
            attend_sem.at[1],
            at(place // NZ, place % NZ, k),
        )
        for place in range(1, NX * NZ)
    ]
    swap = remote(
        attended.at[k], attended.at[k], attend_sem.at[2], attend_sem.at[3], other_core
    )

    def send_attended():
        halves = [
            jnp.concatenate(
                [mixed[pl.ds(8 * head, 8), :] for head in range(4 * half, 4 * half + 4)], axis=1
            )
            for half in range(2)
        ]
        attended[k, here] = jnp.concatenate(halves, axis=0).astype(jnp.bfloat16)
        for copy in gathers:
            copy.start()

    after = (
        None,
        (over_x[0][1].start, zo[0].up_free.start, over_x[1][1].start, zo[1].up_free.start, split_heads),
        (over_x[0][3].start, zo[0].down_free.start, zo[1].down_free.start, zo[0].pass_far),
        (zs[0].start_far, zo[1].pass_far, lambda: x_far(0)),
        (zs[0].up_free.start,),
        (zs[0].down_free.start, lambda: x_up(0)),
        (send_attended, over_x[0][0].start, lambda: send_last(0)),
        (),
    )
    first_row = 3

    def first_core_copy(half):
        columns = pl.ds(HALF * half, HALF)
        return remote(
            part.at[0, pl.ds(given, ROWS), columns],
            from_core.at[0, :, columns],
            send_sem.at[0],
            core_sem.at[SLABS * half],
            other_core,
        )

    def slab_half(slot, half, rows):
        columns = pl.ds(HALF * half, HALF)
        part[slot, rows, columns] = lax.dot_general(
            grads[slot, :, rows], attn[:, columns], (((0,), (0,)), ((), ())), preferred_element_type=jnp.float32
        ).astype(jnp.bfloat16)

    def send_first(half):
        columns = pl.ds(HALF * half, HALF)
        first_core_copy(half).wait_recv()
        for begin in range(0, ROWS, 16):
            rows = pl.ds(pl.multiple_of(own + begin, 16), 16)
            part[0, rows, columns] = part[0, rows, columns] + from_core[0, pl.ds(begin, 16), columns]
        _, first, count, _ = STREAMS[0][2]
        remote(
            own_rows(1, 2, first, count).at[:, columns],
            x_landing(0, 2).at[:, columns],
            send_sem.at[1],
            x_sem.at[0, 2],
            other_x,
        ).start()
        _, first, count, cut = STREAMS[0][0]
        for n, begin, size, device in ((0, 0, cut, up), (1, cut, count - cut, down)):
            remote(
                own_rows(1, 2, first + begin, size).at[:, columns],
                zo[0].far.at[pl.ds(begin, size), columns],
                send_sem.at[3],
                z_sem.at[0, 0, n],
                device,
            ).start()

    grad_loads[0].wait()
    for half in range(2):
        attn_loads[half].wait()
        slab_half(0, half, pl.ds(pl.multiple_of((1 - k) * 256, 128), 384))
        if half == 0:
            pl.semaphore_wait(barrier, 1 + 7 + 3 + 16 - stays.astype(jnp.int32))
            grad_loads[1].start()
        first_core_copy(half).start()
        slab_half(0, half, pl.ds(pl.multiple_of(k * 384, 128), 256))
    grad_loads[2].start()
    for copy in late_loads[:6]:
        copy.start()
    send_first(0)
    grad_loads[1].wait()
    slab_half(1, 0, pl.ds(0, 2 * ROWS))
    send_first(1)
    over_x[1][2].start()
    zo[1].start_far()
    slab_half(1, 1, pl.ds(0, 2 * ROWS))
    core_copy(1).start()
    grad_loads[3].start()

    @pl.loop(2, SLABS + 1)
    def _(step):
        @pl.when(step < SLABS)
        def _():
            pltpu.make_async_copy(
                grad_hbm.at[:, pl.ds(0, 2 * ROWS)], grads.at[step], grad_sem.at[step]
            ).wait()

        for slot in range(4, SLABS):
            @pl.when(step == slot - 2)
            def _():
                grad_loads[slot].start()
                if slot == 6:
                    for copy in late_loads[6:]:
                        copy.start()

        @pl.when(step < SLABS)
        def _():
            part[step] = lax.dot_general(
                grads[step], attn[...], (((0,), (0,)), ((), ())), preferred_element_type=jnp.float32
            ).astype(jnp.bfloat16)
            core_copy(step).start()

        done = step - 1
        core_copy(done).wait_recv()
        rows = pl.ds(own, ROWS)
        part[done, rows, :] = part[done, rows, :] + from_core[done]

        for slot in range(1, SLABS):
            @pl.when(step == slot + 1)
            def _():
                for action in after[slot]:
                    action()

        @pl.when(jnp.logical_and(step >= first_row, step < first_row + 4))
        def _():
            attend(2 * (step - first_row))
            attend(2 * (step - first_row) + 1)

    zs[0].pass_far()
    x_down(0)
    xs[0].pass_far()
    zs[1].start_far()
    x_far(1)
    zs[1].start_free()
    x_up(1)
    over_x[1][3].start()
    over_x[1][0].start()
    send_last(1)
    wait_bytes(attended.at[k, pl.ds(0, 7)], attend_sem.at[1])
    swap.start()
    weights[pl.ds(ROWS, PADDED - ROWS), :] = jnp.zeros((PADDED - ROWS, COLS), jnp.bfloat16)
    wait_bytes(state, load_sem.at[5])

    def adam(first, count, terms):
        @pl.loop(0, count // 16)
        def _(n):
            begin = pl.multiple_of(n * 16, 16)
            rows = pl.ds(pl.multiple_of(first + begin, 16), 16)
            mine = pl.ds(pl.multiple_of(own + first + begin, 16), 16)
            total = part[SLOT[0, 0], mine, :].astype(jnp.float32)
            for term in terms:
                total = total + term[pl.ds(begin, 16), :].astype(jnp.float32)
            grad = total * (1.0 / TOKENS)
            one_new = beta_one * state[1, rows, :] + (1.0 - beta_one) * grad
            two_new = beta_two * state[2, rows, :] + (1.0 - beta_two) * grad * grad
            update = (one_new * (1.0 / bias_one)) / (jnp.sqrt(two_new * (1.0 / bias_two)) + adam_eps)
            master_new = state[0, rows, :] * (1.0 - learn_rate * weight_decay) - learn_rate * update
            one_out[rows, :] = one_new
            two_out[rows, :] = two_new
            master_out[rows, :] = master_new
            weights[rows, :] = master_new.astype(jnp.bfloat16)

    def adam_x(chunk):
        xs[chunk].wait_near()
        over_x[chunk][0].wait_recv()
        _, first, count, _ = STREAMS[chunk][2]
        adam(first, count, (x_landing(chunk, 0), xs[chunk].near.at[0], xs[chunk].near.at[1]))

    def adam_z(chunk):
        zs[chunk].wait_near()
        last_x[chunk].wait_recv()
        _, first, count, _ = STREAMS[chunk][1]
        adam(first, count, (z_landing(chunk), zs[chunk].near.at[0], zs[chunk].near.at[1]))

    def product(first, count):
        halves = [
            lax.dot_general(
                attended[...].reshape(256, HALF),
                weights[pl.ds(first, count), pl.ds(HALF * half, HALF)],
                (((1,), (1,)), ((), ())),
                preferred_element_type=jnp.float32,
            ).reshape(2, 8, 16, count)[:, :, 8 * half : 8 * half + 8, :]
            for half in range(2)
        ]
        return halves[0] + halves[1]

    adam_z(0)
    adam_x(0)
    swap.wait_recv()
    share = product(0, EARLY)
    for place in range(NZ):
        shares[place] = jnp.concatenate(
            [share[core, dx * NZ + place] for dx in range(NX) for core in range(2)], axis=0
        ).astype(jnp.bfloat16)

    for step in (2, 1, 3):
        remote(
            shares.at[lax.rem(z_summed + step, NZ)],
            arrived.at[step - 1],
            share_sem.at[0],
            share_sem.at[1],
            (f, lax.rem(y + step, 4) * 2 + x_hi),
        ).start()

    zs[1].pass_far()
    x_down(1)
    xs[1].pass_far()
    adam_z(1)
    adam_x(1)
    late_shares[...] = product(EARLY, PADDED - EARLY).reshape(16, 8, PADDED - EARLY)

    def late_copy(step):
        target = lax.rem(f + step, 16)
        return remote(
            late_shares.at[lax.rem(target, 2) * 8 + target // 2],
            late_arrived.at[k, t],
            late_sem.at[0],
            late_sem.at[1],
            (target, f // 2),
        )

    for step in range(1, 16):
        late_copy(step).start()

    @pl.when(stays)
    def _():
        pltpu.make_async_copy(
            late_shares.at[k * 8 + f // 2], late_arrived.at[k, t], late_sem.at[1]
        ).start()

    @pl.when(jnp.logical_not(stays))
    def _():
        late_copy(0).start()

    wait_bytes(arrived, share_sem.at[1])
    total = shares[z_summed].astype(jnp.float32)
    for step in range(3):
        total = total + arrived[step].astype(jnp.float32)
    totals[...] = total
    for dx in range(NX):
        for core in range(2):
            remote(
                totals.at[pl.ds(8 * (2 * dx + core), 8)],
                decoded.at[k, x_hi],
                share_sem.at[2],
                share_sem.at[3],
                ((dx * NZ + z_summed) * 2 + core, f // 2),
            ).start()

    wait_bytes(from_core, send_sem.at[0])
    wait_bytes(from_x, send_sem.at[1])
    wait_bytes(from_x_last, send_sem.at[2])
    for number, (near, far) in enumerate(((zo_near, zo_far), (zs_near, zs_far), (xs_near, xs_far))):
        wait_bytes(far, send_sem.at[3 + 2 * number])
        wait_bytes(near, send_sem.at[4 + 2 * number])
    wait_bytes(attended.at[k, pl.ds(0, 7)], attend_sem.at[0])
    swap.wait_send()
    wait_bytes(arrived, share_sem.at[0])
    wait_bytes(decoded, share_sem.at[2])

    @pl.when(stays)
    def _():
        wait_bytes(late_shares.at[pl.ds(0, 15)], late_sem.at[0])

    @pl.when(jnp.logical_not(stays))
    def _():
        wait_bytes(late_shares, late_sem.at[0])

    wait_bytes(decoded, share_sem.at[3])
    decoded_out[:, :, pl.ds(0, EARLY)] = decoded[:, 0] + decoded[:, 1]
    wait_bytes(late_arrived, late_sem.at[1])
    decoded_out[:, :, pl.ds(EARLY, PADDED - EARLY)] = jnp.sum(late_arrived[...], axis=1)


def write_kernel(master, one, two, decoded, master_out, one_out, two_out, decoded_out, rounded, sems):
    pairs = ((master, master_out), (one, one_out), (two, two_out))
    for piece in range(4):
        rows = pl.ds(ROWS // 4 * piece, ROWS // 4)
        for n, (src, dst) in enumerate(pairs):
            pltpu.make_async_copy(src.at[rows], dst.at[rows], sems.at[n]).start()
    rounded[...] = jnp.concatenate(
        [decoded[core, :, :ROWS] for core in range(2)], axis=1
    ).astype(jnp.bfloat16)
    last = pltpu.make_async_copy(rounded, decoded_out, sems.at[3])
    last.start()
    for n, (src, dst) in enumerate(pairs):
        pltpu.make_async_copy(src, dst, sems.at[n]).wait()
    last.wait()


def shards(*args):
    bf16, f32 = jnp.bfloat16, jnp.float32
    vmem = pl.BlockSpec(memory_space=pltpu.VMEM)
    anywhere = pl.BlockSpec(memory_space=pl.ANY)
    results = pl.pallas_call(
        kernel,
        out_shape=(
            pltpu.VMEM((ROWS, COLS), f32),
            pltpu.VMEM((ROWS, COLS), f32),
            pltpu.VMEM((ROWS, COLS), f32),
            pltpu.VMEM((2, 8, PADDED), f32),
        ),
        in_specs=[anywhere] * 11,
        out_specs=(vmem,) * 4,
        scratch_shapes=[
            pltpu.VMEM((1024, COLS), bf16),
            pltpu.VMEM((SLABS, 1024, 2 * ROWS), bf16),
            pltpu.VMEM((SLABS, 2 * ROWS, COLS), bf16),
            pltpu.VMEM((SLABS, ROWS, COLS), bf16),
            pltpu.VMEM((NZ, X_TOTAL, COLS), bf16),
            pltpu.VMEM((Z_TOTAL, COLS), bf16),
            pltpu.VMEM((2, Z_TOTAL, COLS), bf16),
            pltpu.VMEM((Z_TOTAL, COLS), bf16),
            pltpu.VMEM((2, Z_TOTAL, COLS), bf16),
            pltpu.VMEM((Z_TOTAL, COLS), bf16),
            pltpu.VMEM((2, X_TOTAL, COLS), bf16),
            pltpu.VMEM((X_TOTAL, COLS), bf16),
            pltpu.VMEM((3, ROWS, COLS), f32),
            pltpu.VMEM((8, 1024), bf16),
            pltpu.VMEM((8, HEAD_SIZE), bf16),
            pltpu.VMEM((8, HEAD_SIZE), bf16),
            pltpu.VMEM((2, 8, 1, CACHE_SLOTS, HEAD_SIZE), bf16),
            pltpu.SMEM((8,), jnp.int32),
            pltpu.VMEM((PADDED, COLS), bf16),
            pltpu.VMEM((64, HEAD_SIZE), f32),
            pltpu.VMEM((64, HEAD_SIZE), f32),
            pltpu.VMEM((2, 8, HEAD_SIZE), f32),
            pltpu.VMEM((2, 8, 16, HALF), bf16),
            pltpu.VMEM((NZ, 32, EARLY), bf16),
            pltpu.VMEM((3, 32, EARLY), bf16),
            pltpu.VMEM((32, EARLY), f32),
            pltpu.VMEM((2, 2, 8, EARLY), f32),
            pltpu.VMEM((16, 8, PADDED - EARLY), f32),
            pltpu.VMEM((2, 8, 8, PADDED - EARLY), f32),
            pltpu.SemaphoreType.DMA((6,)),
            pltpu.SemaphoreType.DMA((2,)),
            pltpu.SemaphoreType.DMA((SLABS,)),
            pltpu.SemaphoreType.DMA((SLABS + 1,)),
            pltpu.SemaphoreType.DMA((2, NZ + 1)),
            pltpu.SemaphoreType.DMA((2, 3, 3)),
            pltpu.SemaphoreType.DMA((4,)),
            pltpu.SemaphoreType.DMA((4,)),
            pltpu.SemaphoreType.DMA((2,)),
            pltpu.SemaphoreType.DMA((9,)),
        ],
        compiler_params=pltpu.CompilerParams(
            collective_id=0, has_side_effects=True, vmem_limit_bytes=50 << 20
        ),
        cost_estimate=pl.CostEstimate(
            flops=2 * 1024 * 1024 * 5120, bytes_accessed=24 << 20, transcendentals=1 << 19
        ),
    )(*(pltpu.with_memory_space_constraint(arg, pltpu.HBM) for arg in args))
    return pl.pallas_call(
        write_kernel,
        out_shape=(
            jax.ShapeDtypeStruct((ROWS, COLS), f32),
            jax.ShapeDtypeStruct((ROWS, COLS), f32),
            jax.ShapeDtypeStruct((ROWS, COLS), f32),
            jax.ShapeDtypeStruct((8, 2 * ROWS), bf16),
        ),
        in_specs=[vmem] * 4,
        out_specs=(anywhere,) * 4,
        scratch_shapes=[pltpu.VMEM((8, 2 * ROWS), bf16), pltpu.SemaphoreType.DMA((4,))],
        compiler_params=pltpu.CompilerParams(vmem_limit_bytes=8 << 20),
        cost_estimate=pl.CostEstimate(flops=0, bytes_accessed=8 << 20, transcendentals=0),
    )(*results)


def solution(mesh):
    placed = (
        P("fsdp", "tp"),
        P("fsdp", None),
        P("fsdp", "tp"),
        P("fsdp", "tp"),
        P("fsdp", "tp"),
        P("fsdp", "tp"),
        P("fsdp", "tp"),
        P("fsdp", "tp"),
        P("fsdp", "tp", None, None),
        P("fsdp", "tp", None, None),
        P("fsdp"),
    )
    return jax.shard_map(
        shards,
        mesh=mesh,
        in_specs=placed,
        out_specs=(P("fsdp", "tp"), P("fsdp", "tp"), P("fsdp", "tp"), P("fsdp", "tp")),
        check_vma=False,
    )
```

time: 60.1 us -> 58.4 us (0.972)
  Pallas kernels: 59.3 us -> 57.6 us
    pallas_call x1, Pallas kernels: 57.4 us -> 55.6 us  [shards(): pl.pallas_call(kernel, out_shape=(pltpu.VMEM((ROWS, COLS), f32), pltpu.VM...]
where the time goes in v3:
time: 58.4 us; the launch traced here: 58.2 us
  Pallas kernels  57.6 us (99%)
  between operations  0.64 us (1%)
    pallas_call x1, Pallas kernels, shards(): pl.pallas_call(kernel, out_shape=(pltpu.VMEM((ROWS, COLS), f32), pltpu.VM...  55.6 us
    pallas_call x1, Pallas kernels, shards(): pl.pallas_call(write_kernel, out_shape=(jax.ShapeDtypeStruct((ROWS, COLS)...  1.95 us

profile of v3, /device:TPU:1, one launch (start us, length us, event | category | flops | bytes accessed | tf_op | source)
XLA Modules:
  0.0 58.2 jit_solution(11658784383517462351)
XLA Ops:
  0.6 55.6 %shard_map.138 = (f32[320,1024]{1,0:T(8,128)S(1)}, f32[320,1024]{1,0:T(8,128)S(1)}, f32[320,1024]{1,0:T(8,128)S(1)}, f32[2,8,384]{2,1,0:T(8,128)S(1)}) custom-call(bf16[1024,1024]{1,0:T(8,128)(2,1)} %attn_hbm.1, bf16[1024,5120]{1,0:T(8,128)(2,1)} %grad_hbm.1, f32[320,1024]{1,0:T(8,128)} %master_hbm.1, f32[320,1024]{1,0:T(8,128)} %one_hbm.1, ...), custom_call_target="tpu_custom_call" | custom-call | flops 10737418240 | bytes 25165824 | tf_op jit(solution)/shard_map/pallas_call | solution.py:651
  56.3 1.9 %shard_map.139 = (f32[320,1024]{1,0:T(8,128)}, f32[320,1024]{1,0:T(8,128)}, f32[320,1024]{1,0:T(8,128)}, bf16[8,640]{1,0:T(8,128)(2,1)}) custom-call(f32[320,1024]{1,0:T(8,128)S(1)} %get-tuple-element.8.master, f32[320,1024]{1,0:T(8,128)S(1)} %get-tuple-element.9.one, f32[320,1024]{1,0:T(8,128)S(1)} %get-tuple-element.10.two, ...), custom_call_target="tpu_custom_call" | custom-call | bytes 8388608 | tf_op jit(solution)/shard_map/pallas_call | solution.py:709

commit v4 on v3

--- a/solution.py
+++ b/solution.py
@@ -92,6 +92,7 @@
     share_sem,
     late_sem,
     send_sem,
+    news_sem,
 ):
     f = lax.axis_index("fsdp")
     t = lax.axis_index("tp")
@@ -152,25 +153,18 @@
         ).start()
 
     barrier = pltpu.get_barrier_semaphore()
-
-    def greet(device):
+    up_y = (f, lax.rem(y + 1, 4) * 2 + x_hi)
+    down_y = (f, lax.rem(y + 3, 4) * 2 + x_hi)
+    across_x = (chip(1, 0) * 2 + k, y * 2 + 1 - x_hi)
+    neighbours = (other_core, other_x, up, down, up_y, down_y, across_x)
+    for device in neighbours:
         pl.semaphore_signal(barrier, inc=1, device_id=device, device_id_type=MESH)
-
-    greet(other_core)
-    for place in range(1, NX * NZ):
-        greet(at(place // NZ, place % NZ, k))
-    for step in range(1, 4):
-        greet((f, lax.rem(y + step, 4) * 2 + x_hi))
     stays = t == f // 2
-    for core in range(2):
-        for step in range(8):
-            source = (2 * t + core, lax.rem(t + step, 8))
-            if step == 0:
-                @pl.when(jnp.logical_not(jnp.logical_and(stays, k == core)))
-                def _():
-                    greet(source)
-            else:
-                greet(source)
+
+    def tell(n, *devices):
+        for device in devices:
+            pl.semaphore_signal(news_sem.at[n], inc=1, device_id=device, device_id_type=MESH)
+
     attn_loads[1].start()
 
     def remote(src, dst, send, recv, device):
@@ -299,11 +293,12 @@
         add_x(chunk, 3)
         xs[chunk].down_free.start()
 
-    def send_last(chunk):
+    def send_last(chunk, start=True):
         stream = zo[chunk]
         stream.wait_near()
         add_own(1, 0, stream.first, stream.count, stream.near.at[0], stream.near.at[1])
-        last_x[chunk].start()
+        if start:
+            last_x[chunk].start()
 
     def split_heads():
         for copy in late_loads[:4]:
@@ -376,7 +371,7 @@
         (zs[0].start_far, zo[1].pass_far, lambda: x_far(0)),
         (zs[0].up_free.start,),
         (zs[0].down_free.start, lambda: x_up(0)),
-        (send_attended, over_x[0][0].start, lambda: send_last(0)),
+        (lambda: send_last(0, False), send_attended, over_x[0][0].start, last_x[0].start),
         (),
     )
     first_row = 3
@@ -426,7 +421,7 @@
         attn_loads[half].wait()
         slab_half(0, half, pl.ds(pl.multiple_of((1 - k) * 256, 128), 384))
         if half == 0:
-            pl.semaphore_wait(barrier, 1 + 7 + 3 + 16 - stays.astype(jnp.int32))
+            pl.semaphore_wait(barrier, len(neighbours))
             grad_loads[1].start()
         first_core_copy(half).start()
         slab_half(0, half, pl.ds(pl.multiple_of(k * 384, 128), 256))
@@ -482,6 +477,7 @@
             attend(2 * (step - first_row))
             attend(2 * (step - first_row) + 1)
 
+    tell(0, up_y, down_y)
     zs[0].pass_far()
     x_down(0)
     xs[0].pass_far()
@@ -492,8 +488,12 @@
     over_x[1][3].start()
     over_x[1][0].start()
     send_last(1)
+    pl.semaphore_wait(news_sem.at[0], 2)
+    tell(1, up_y, down_y)
     wait_bytes(attended.at[k, pl.ds(0, 7)], attend_sem.at[1])
     swap.start()
+    pl.semaphore_wait(news_sem.at[1], 2)
+    tell(2, across_x)
     weights[pl.ds(ROWS, PADDED - ROWS), :] = jnp.zeros((PADDED - ROWS, COLS), jnp.bfloat16)
     wait_bytes(state, load_sem.at[5])
 
@@ -544,6 +544,7 @@
     adam_x(0)
     swap.wait_recv()
     share = product(0, EARLY)
+    pl.semaphore_wait(news_sem.at[2], 1)
     for place in range(NZ):
         shares[place] = jnp.concatenate(
             [share[core, dx * NZ + place] for dx in range(NX) for core in range(2)], axis=0
@@ -698,6 +699,7 @@
             pltpu.SemaphoreType.DMA((4,)),
             pltpu.SemaphoreType.DMA((2,)),
             pltpu.SemaphoreType.DMA((9,)),
+            pltpu.SemaphoreType.REGULAR((3,)),
         ],
         compiler_params=pltpu.CompilerParams(
             collective_id=0, has_side_effects=True, vmem_limit_bytes=50 << 20

time: 58.4 us -> 57.9 us (level)
  no operation moved by 1% of the time
where the time goes in v4:
time: 57.9 us; the launch traced here: 57.7 us
  Pallas kernels  57.1 us (99%)
  between operations  0.64 us (1%)
    pallas_call x1, Pallas kernels, shards(): pl.pallas_call(kernel, out_shape=(pltpu.VMEM((ROWS, COLS), f32), pltpu.VM...  55.1 us
    pallas_call x1, Pallas kernels, shards(): pl.pallas_call(write_kernel, out_shape=(jax.ShapeDtypeStruct((ROWS, COLS)...  1.95 us

profile of v4, /device:TPU:1, one launch (start us, length us, event | category | flops | bytes accessed | tf_op | source)
XLA Modules:
  0.0 57.7 jit_solution(10237880332197638440)
XLA Ops:
  0.6 55.1 %shard_map.138 = (f32[320,1024]{1,0:T(8,128)S(1)}, f32[320,1024]{1,0:T(8,128)S(1)}, f32[320,1024]{1,0:T(8,128)S(1)}, f32[2,8,384]{2,1,0:T(8,128)S(1)}) custom-call(bf16[1024,1024]{1,0:T(8,128)(2,1)} %attn_hbm.1, bf16[1024,5120]{1,0:T(8,128)(2,1)} %grad_hbm.1, f32[320,1024]{1,0:T(8,128)} %master_hbm.1, f32[320,1024]{1,0:T(8,128)} %one_hbm.1, ...), custom_call_target="tpu_custom_call" | custom-call | flops 10737418240 | bytes 25165824 | tf_op jit(solution)/shard_map/pallas_call | solution.py:652
  55.8 1.9 %shard_map.139 = (f32[320,1024]{1,0:T(8,128)}, f32[320,1024]{1,0:T(8,128)}, f32[320,1024]{1,0:T(8,128)}, bf16[8,640]{1,0:T(8,128)(2,1)}) custom-call(f32[320,1024]{1,0:T(8,128)S(1)} %get-tuple-element.8.master, f32[320,1024]{1,0:T(8,128)S(1)} %get-tuple-element.9.one, f32[320,1024]{1,0:T(8,128)S(1)} %get-tuple-element.10.two, ...), custom_call_target="tpu_custom_call" | custom-call | bytes 8388608 | tf_op jit(solution)/shard_map/pallas_call | solution.py:711

commit v5 on v4

--- a/solution.py
+++ b/solution.py
@@ -542,6 +542,8 @@
 
     adam_z(0)
     adam_x(0)
+    zs[1].pass_far()
+    x_down(1)
     swap.wait_recv()
     share = product(0, EARLY)
     pl.semaphore_wait(news_sem.at[2], 1)
@@ -559,35 +561,9 @@
             (f, lax.rem(y + step, 4) * 2 + x_hi),
         ).start()
 
-    zs[1].pass_far()
-    x_down(1)
     xs[1].pass_far()
     adam_z(1)
     adam_x(1)
-    late_shares[...] = product(EARLY, PADDED - EARLY).reshape(16, 8, PADDED - EARLY)
-
-    def late_copy(step):
-        target = lax.rem(f + step, 16)
-        return remote(
-            late_shares.at[lax.rem(target, 2) * 8 + target // 2],
-            late_arrived.at[k, t],
-            late_sem.at[0],
-            late_sem.at[1],
-            (target, f // 2),
-        )
-
-    for step in range(1, 16):
-        late_copy(step).start()
-
-    @pl.when(stays)
-    def _():
-        pltpu.make_async_copy(
-            late_shares.at[k * 8 + f // 2], late_arrived.at[k, t], late_sem.at[1]
-        ).start()
-
-    @pl.when(jnp.logical_not(stays))
-    def _():
-        late_copy(0).start()
 
     wait_bytes(arrived, share_sem.at[1])
     total = shares[z_summed].astype(jnp.float32)
@@ -603,6 +579,31 @@
                 share_sem.at[3],
                 ((dx * NZ + z_summed) * 2 + core, f // 2),
             ).start()
+
+    late_shares[...] = product(EARLY, PADDED - EARLY).reshape(16, 8, PADDED - EARLY)
+
+    def late_copy(step):
+        target = lax.rem(f + step, 16)
+        return remote(
+            late_shares.at[lax.rem(target, 2) * 8 + target // 2],
+            late_arrived.at[k, t],
+            late_sem.at[0],
+            late_sem.at[1],
+            (target, f // 2),
+        )
+
+    for step in range(1, 16):
+        late_copy(step).start()
+
+    @pl.when(stays)
+    def _():
+        pltpu.make_async_copy(
+            late_shares.at[k * 8 + f // 2], late_arrived.at[k, t], late_sem.at[1]
+        ).start()
+
+    @pl.when(jnp.logical_not(stays))
+    def _():
+        late_copy(0).start()
 
     wait_bytes(from_core, send_sem.at[0])
     wait_bytes(from_x, send_sem.at[1])

time: 57.9 us -> 56.9 us (0.983)
  Pallas kernels: 57.1 us -> 56.1 us
    pallas_call x1, Pallas kernels: 55.1 us -> 54.2 us  [shards(): pl.pallas_call(kernel, out_shape=(pltpu.VMEM((ROWS, COLS), f32), pltpu.VM...]
where the time goes in v5:
time: 56.9 us; the launch traced here: 56.8 us
  Pallas kernels  56.1 us (99%)
  between operations  0.64 us (1%)
    pallas_call x1, Pallas kernels, shards(): pl.pallas_call(kernel, out_shape=(pltpu.VMEM((ROWS, COLS), f32), pltpu.VM...  54.2 us
    pallas_call x1, Pallas kernels, shards(): pl.pallas_call(write_kernel, out_shape=(jax.ShapeDtypeStruct((ROWS, COLS)...  1.95 us

profile of v5, /device:TPU:1, one launch (start us, length us, event | category | flops | bytes accessed | tf_op | source)
XLA Modules:
  0.0 56.8 jit_solution(10653397800004182073)
XLA Ops:
  0.6 54.2 %shard_map.138 = (f32[320,1024]{1,0:T(8,128)S(1)}, f32[320,1024]{1,0:T(8,128)S(1)}, f32[320,1024]{1,0:T(8,128)S(1)}, f32[2,8,384]{2,1,0:T(8,128)S(1)}) custom-call(bf16[1024,1024]{1,0:T(8,128)(2,1)} %attn_hbm.1, bf16[1024,5120]{1,0:T(8,128)(2,1)} %grad_hbm.1, f32[320,1024]{1,0:T(8,128)} %master_hbm.1, f32[320,1024]{1,0:T(8,128)} %one_hbm.1, ...), custom_call_target="tpu_custom_call" | custom-call | flops 10737418240 | bytes 25165824 | tf_op jit(solution)/shard_map/pallas_call | solution.py:653
  54.8 1.9 %shard_map.139 = (f32[320,1024]{1,0:T(8,128)}, f32[320,1024]{1,0:T(8,128)}, f32[320,1024]{1,0:T(8,128)}, bf16[8,640]{1,0:T(8,128)(2,1)}) custom-call(f32[320,1024]{1,0:T(8,128)S(1)} %get-tuple-element.8.master, f32[320,1024]{1,0:T(8,128)S(1)} %get-tuple-element.9.one, f32[320,1024]{1,0:T(8,128)S(1)} %get-tuple-element.10.two, ...), custom_call_target="tpu_custom_call" | custom-call | bytes 8388608 | tf_op jit(solution)/shard_map/pallas_call | solution.py:712

commit v6 on v5

--- a/solution.py
+++ b/solution.py
@@ -28,7 +28,7 @@
 SLABS = len(ORDER)
 SLOT = {place: slot for slot, place in enumerate(ORDER)}
 STREAMS = (
-    ((1, 112, 144, 80), (0, 112, 144, 80), (0, 0, 112, 48)),
+    ((1, 112, 144, 80), (0, 112, 144, 96), (0, 0, 112, 48)),
     ((1, 288, 32, 16), (0, 288, 32, 16), (0, 256, 32, 16)),
 )
 Z_TOTAL = sum(chunk[0][2] for chunk in STREAMS)

time: 56.9 us -> 56.6 us (level)
  no operation moved by 1% of the time
where the time goes in v6:
time: 56.6 us; the launch traced here: 56.5 us
  Pallas kernels  55.8 us (99%)
  between operations  0.64 us (1%)
    pallas_call x1, Pallas kernels, shards(): pl.pallas_call(kernel, out_shape=(pltpu.VMEM((ROWS, COLS), f32), pltpu.VM...  53.9 us
    pallas_call x1, Pallas kernels, shards(): pl.pallas_call(write_kernel, out_shape=(jax.ShapeDtypeStruct((ROWS, COLS)...  1.95 us

profile of v6, /device:TPU:1, one launch (start us, length us, event | category | flops | bytes accessed | tf_op | source)
XLA Modules:
  0.0 56.5 jit_solution(12874242040669427942)
XLA Ops:
  0.6 53.9 %shard_map.138 = (f32[320,1024]{1,0:T(8,128)S(1)}, f32[320,1024]{1,0:T(8,128)S(1)}, f32[320,1024]{1,0:T(8,128)S(1)}, f32[2,8,384]{2,1,0:T(8,128)S(1)}) custom-call(bf16[1024,1024]{1,0:T(8,128)(2,1)} %attn_hbm.1, bf16[1024,5120]{1,0:T(8,128)(2,1)} %grad_hbm.1, f32[320,1024]{1,0:T(8,128)} %master_hbm.1, f32[320,1024]{1,0:T(8,128)} %one_hbm.1, ...), custom_call_target="tpu_custom_call" | custom-call | flops 10737418240 | bytes 25165824 | tf_op jit(solution)/shard_map/pallas_call | solution.py:653
  54.5 1.9 %shard_map.139 = (f32[320,1024]{1,0:T(8,128)}, f32[320,1024]{1,0:T(8,128)}, f32[320,1024]{1,0:T(8,128)}, bf16[8,640]{1,0:T(8,128)(2,1)}) custom-call(f32[320,1024]{1,0:T(8,128)S(1)} %get-tuple-element.8.master, f32[320,1024]{1,0:T(8,128)S(1)} %get-tuple-element.9.one, f32[320,1024]{1,0:T(8,128)S(1)} %get-tuple-element.10.two, ...), custom_call_target="tpu_custom_call" | custom-call | bytes 8388608 | tf_op jit(solution)/shard_map/pallas_call | solution.py:712

commit v7 on v6

--- a/solution.py
+++ b/solution.py
@@ -582,8 +582,8 @@
 
     late_shares[...] = product(EARLY, PADDED - EARLY).reshape(16, 8, PADDED - EARLY)
 
-    def late_copy(step):
-        target = lax.rem(f + step, 16)
+    def late_copy(dx, dz, core):
+        target = chip(dx, dz) * 2 + lax.rem(k + core, 2)
         return remote(
             late_shares.at[lax.rem(target, 2) * 8 + target // 2],
             late_arrived.at[k, t],
@@ -592,8 +592,9 @@
             (target, f // 2),
         )
 
-    for step in range(1, 16):
-        late_copy(step).start()
+    places = [(dx, dz, core) for dz in (2, 1, 3, 0) for dx in (1, 0) for core in (1, 0)]
+    for place in places[:-1]:
+        late_copy(*place).start()
 
     @pl.when(stays)
     def _():
@@ -603,7 +604,7 @@
 
     @pl.when(jnp.logical_not(stays))
     def _():
-        late_copy(0).start()
+        late_copy(*places[-1]).start()
 
     wait_bytes(from_core, send_sem.at[0])
     wait_bytes(from_x, send_sem.at[1])

time: 56.6 us -> 57 us (level)
  no operation moved by 1% of the time
where the time goes in v7:
time: 57 us; the launch traced here: 56.9 us
  Pallas kernels  56.2 us (99%)
  between operations  0.64 us (1%)
    pallas_call x1, Pallas kernels, shards(): pl.pallas_call(kernel, out_shape=(pltpu.VMEM((ROWS, COLS), f32), pltpu.VM...  54.3 us
    pallas_call x1, Pallas kernels, shards(): pl.pallas_call(write_kernel, out_shape=(jax.ShapeDtypeStruct((ROWS, COLS)...  1.95 us

profile of v7, /device:TPU:1, one launch (start us, length us, event | category | flops | bytes accessed | tf_op | source)
XLA Modules:
  0.0 56.9 jit_solution(17058378745016531163)
XLA Ops:
  0.6 54.3 %shard_map.138 = (f32[320,1024]{1,0:T(8,128)S(1)}, f32[320,1024]{1,0:T(8,128)S(1)}, f32[320,1024]{1,0:T(8,128)S(1)}, f32[2,8,384]{2,1,0:T(8,128)S(1)}) custom-call(bf16[1024,1024]{1,0:T(8,128)(2,1)} %attn_hbm.1, bf16[1024,5120]{1,0:T(8,128)(2,1)} %grad_hbm.1, f32[320,1024]{1,0:T(8,128)} %master_hbm.1, f32[320,1024]{1,0:T(8,128)} %one_hbm.1, ...), custom_call_target="tpu_custom_call" | custom-call | flops 10737418240 | bytes 25165824 | tf_op jit(solution)/shard_map/pallas_call | solution.py:654
  54.9 1.9 %shard_map.139 = (f32[320,1024]{1,0:T(8,128)}, f32[320,1024]{1,0:T(8,128)}, f32[320,1024]{1,0:T(8,128)}, bf16[8,640]{1,0:T(8,128)(2,1)}) custom-call(f32[320,1024]{1,0:T(8,128)S(1)} %get-tuple-element.8.master, f32[320,1024]{1,0:T(8,128)S(1)} %get-tuple-element.9.one, f32[320,1024]{1,0:T(8,128)S(1)} %get-tuple-element.10.two, ...), custom_call_target="tpu_custom_call" | custom-call | bytes 8388608 | tf_op jit(solution)/shard_map/pallas_call | solution.py:713
